TPU v7x, 256 devices: a whole 4x4x8 slice. The times are simulated.
256 devices in a mesh: fsdp: 64 (over x, z, core), group: 4 (over y).
Axes of the slice: x: 4, y: 4, z: 8, core: 2. Of those that a mesh axis runs over, the one named last changes fastest.
Arguments:
- gradient: bfloat16 [16, 512, 8192], P(None, 'fsdp', 'group')
- second_moment: bfloat16 [16, 512, 8192], P(None, 'fsdp', 'group'), may hold values from 0.049804688 to 5
- left_root: bfloat16 [64, 4, 2, 512, 512], P('fsdp', 'group')
- right_root: bfloat16 [64, 4, 2, 512, 512], P('fsdp', 'group')
- block_owner: int32 [256], replicated, may hold values from 0 to 63, as said below
- row_offset: int32 [256], replicated, may hold values from 0 to 7680, as said below
- col_offset: int32 [256], replicated, may hold values from 0 to 7680, as said below
Outputs:
- update: bfloat16 [16, 512, 8192], P(None, 'fsdp')
- new_moment: bfloat16 [16, 512, 8192], P(None, 'fsdp', 'group')
- left_stat: float32 [64, 4, 2, 512, 512], P('fsdp', 'group')
- right_stat: float32 [64, 4, 2, 512, 512], P('fsdp', 'group')
Inputs may be any that keep to these rules, and one draw needn't show every extreme that they name: row_offset and col_offset are multiples of 512; together they name each block position of the window exactly once. `col_offset`: see row_offset. `block_owner`: in each of the 4 column ranges, one owner holds at most 2 of that range's blocks; with m blocks in a range, m // 4 owners hold exactly 2 and m - 2 * (m // 4) further owners hold one each.
All inputs are finite; a program needn't handle non-finite values.
Results may differ from a plain program's by a relative error of at most 0.0049.
Values may be sent and summed in bfloat16 or wider, within the bound.
A program may use at most 64 MiB of HBM per device.

v0:
```python
import jax
import jax.numpy as jnp
from jax import lax
from jax.sharding import PartitionSpec as P


def body(gradient, second_moment, left_root, right_root, block_owner, row_offset, col_offset):
    fsdp_count = lax.axis_size("fsdp")
    range_self = lax.axis_index("group")
    band_count, rows_dev, width_dev = gradient.shape
    tile_size = left_root.shape[-1]
    slot_count = left_root.shape[2]
    per_range = width_dev // tile_size
    piece_count = band_count * per_range
    grad_wide = gradient.astype(jnp.float32)
    new_moment = (0.95 * second_moment.astype(jnp.float32) + 0.05 * grad_wide * grad_wide).astype(
        jnp.bfloat16
    )
    adam_dir = grad_wide / (jnp.sqrt(new_moment.astype(jnp.float32)) + 1e-08)
    block_count = block_owner.shape[0]
    block_band = row_offset // tile_size
    block_col = col_offset // tile_size
    col_range = block_col // per_range
    local_col = block_col % per_range
    position = jnp.arange(block_count, dtype=jnp.int32)
    earlier = (
        (col_range[:, None] == col_range[None, :])
        & (block_owner[:, None] == block_owner[None, :])
        & (position[None, :] < position[:, None])
    )
    slot_index = jnp.sum(earlier.astype(jnp.int32), axis=1)
    in_range = col_range == range_self
    piece_index = block_band * per_range + local_col
    owner_key = slot_index * fsdp_count + block_owner
    key_values = jnp.arange(slot_count * fsdp_count, dtype=jnp.int32)
    key_match = (owner_key[None, :] == key_values[:, None]) & in_range[None, :]
    key_filled = jnp.any(key_match, axis=1)
    piece_of_key = jnp.sum(jnp.where(key_match, piece_index[None, :], 0), axis=1)
    grad_split = gradient.reshape(band_count, rows_dev, per_range, tile_size)
    outgoing = grad_split[piece_of_key // per_range, :, piece_of_key % per_range, :]
    outgoing = jnp.where(key_filled[:, None, None], outgoing, jnp.zeros_like(outgoing))
    outgoing = outgoing.reshape(slot_count, fsdp_count * rows_dev, tile_size)
    blocks_in = lax.all_to_all(outgoing, "fsdp", split_axis=1, concat_axis=1, tiled=True)
    stat_left = (
        jnp.einsum("sik,sjk->sij", blocks_in, blocks_in, preferred_element_type=jnp.float32)
        / tile_size
    )
    stat_right = (
        jnp.einsum("ski,skj->sij", blocks_in, blocks_in, preferred_element_type=jnp.float32)
        / tile_size
    )
    half_done = jnp.einsum(
        "sij,sjk->sik", left_root[0, 0], blocks_in, preferred_element_type=jnp.float32
    ).astype(jnp.bfloat16)
    precond = jnp.einsum(
        "sij,sjk->sik", half_done, right_root[0, 0], preferred_element_type=jnp.float32
    )
    p_mean = jnp.mean(precond * precond, axis=(1, 2))
    adam_split = adam_dir.reshape(band_count, rows_dev, per_range, tile_size)
    adam_partial = jnp.sum(adam_split * adam_split, axis=(1, 3))
    adam_total = lax.psum(adam_partial, "fsdp")
    adam_mean = adam_total.reshape(-1) / (tile_size * tile_size)
    piece_values = jnp.arange(piece_count, dtype=jnp.int32)
    piece_match = (piece_index[None, :] == piece_values[:, None]) & in_range[None, :]
    key_of_piece = jnp.sum(jnp.where(piece_match, owner_key[None, :], 0), axis=1)
    spread_mean = jnp.broadcast_to(p_mean[:, None], (slot_count, fsdp_count))
    returned, mean_back = (
        lax.all_to_all(precond, "fsdp", split_axis=1, concat_axis=1, tiled=True),
        lax.all_to_all(spread_mean, "fsdp", split_axis=1, concat_axis=1, tiled=True),
    )
    returned = returned.reshape(slot_count * fsdp_count, rows_dev, tile_size)
    picked = returned[key_of_piece]
    picked_mean = mean_back.reshape(-1)[key_of_piece]
    graft_scale = jnp.sqrt(adam_mean / (picked_mean + 1e-06))
    pieces_out = (picked * graft_scale[:, None, None]).astype(jnp.bfloat16)
    local_update = (
        pieces_out.reshape(band_count, per_range, rows_dev, tile_size)
        .transpose(0, 2, 1, 3)
        .reshape(band_count, rows_dev, width_dev)
    )
    update = lax.all_gather(local_update, "group", axis=2, tiled=True)
    left_stat = stat_left.reshape(1, 1, slot_count, tile_size, tile_size)
    right_stat = stat_right.reshape(1, 1, slot_count, tile_size, tile_size)
    return (update, new_moment, left_stat, right_stat)


def solution(mesh):
    placed = (
        P(None, "fsdp", "group"),
        P(None, "fsdp", "group"),
        P("fsdp", "group", None, None, None),
        P("fsdp", "group", None, None, None),
        P(),
        P(),
        P(),
    )
    return jax.shard_map(
        body,
        mesh=mesh,
        in_specs=placed,
        out_specs=(
            P(None, "fsdp", None),
            P(None, "fsdp", "group"),
            P("fsdp", "group", None, None, None),
            P("fsdp", "group", None, None, None),
        ),
        check_vma=False,
    )
```

profile of v0, /device:TPU:1, one launch (start us, length us, event | category | flops | bytes accessed | tf_op | source)
XLA Modules:
  0.0 292.6 jit_solution(16971243859179515916)
XLA Ops:
  7.2 0.0 copy-start
  7.2 0.8 broadcast_compare_fusion
  8.0 1.0 convert_reduce_fusion
  8.9 0.7 fusion.15
  9.7 0.1 fusion.12
  9.8 0.1 select_reduce_fusion
  9.9 0.1 broadcast_in_dim.42
  10.0 0.1 broadcast_in_dim.43
  10.1 0.1 broadcast_in_dim.44
  10.2 1.9 gather_fusion
  12.1 0.2 bitcast_select_fusion
  12.3 1.1 copy.44
  13.4 41.3 %all_to_all.16 = bf16[2,512,512]{2,0,1:T(2,128)(2,1)S(1)} all-to-all(bf16[2,512,512]{2,0,1:T(2,128)(2,1)S(1)} %copy.44), channel_id=1, replica_groups=mesh['fsdp'=64,'group'=4] {'fsdp'}, dimensions={1} | all-to-all | bytes 2097152 | tf_op jit(solution)/shard_map/all_to_all | solution.py:43
  54.7 1.4 copy.45
  56.2 0.0 copy-done
  56.2 0.0 copy-start.2
  56.2 4.2 %multiply_reduce_fusion = (f32[2]{0:T(128)S(1)}, f32[2,512,512]{2,1,0:T(8,128)}) fusion(bf16[1,1,2,512,512]{4,3,2,1,0:T(8,128)(2,1)S(1)} %copy-done, bf16[2,512,512]{1,2,0:T(8,128)(2,1)S(1)} %copy.45, bf16[1,1,2,512,512]{4,3,2,1,0:T(8,128)(2,1)} %param.9), kind=kOutput, calls=%fused_computation.5 | convolution fusion | flops 1075314688 | bytes 5242888 | tf_op jit(solution)/shard_map/sij,sjk->sik/dot_general | solution.py:55
  60.4 0.0 copy-done.2
  60.4 0.6 broadcast_in_dim.76
  61.1 6.2 %all-to-all-start.2 = ((f32[2,64,1]{0,2,1:T(1,128)}), f32[2,64,1]{0,2,1:T(1,128)S(1)}, u32[]{:S(2)}, u32[]{:S(2)}) async-start(f32[2,64,1]{0,2,1:T(1,128)} %broadcast_in_dim.76), calls=%async_computation.2 | async-start | bytes 65536 | tf_op jit(solution)/shard_map/all_to_all | solution.py:69
  67.3 4.5 %copy.47 = f32[2,512,512]{2,0,1:T(2,128)} copy(f32[2,512,512]{2,1,0:T(8,128)} %get-tuple-element.10) | data formatting | bytes 4194304 | tf_op jit(solution)/shard_map/sij,sjk->sik/dot_general | solution.py:55
  71.8 4.7 %all-to-all-done.2 = f32[2,64,1]{0,2,1:T(1,128)S(1)} async-done(((f32[2,64,1]{0,2,1:T(1,128)}), f32[2,64,1]{0,2,1:T(1,128)S(1)}, u32[]{:S(2)}, u32[]{:S(2)}) %all-to-all-start.2) | async-done | bytes 544 | tf_op jit(solution)/shard_map/all_to_all | solution.py:69
  76.5 6.0 %all-to-all-start.1 = ((f32[2,512,512]{2,0,1:T(2,128)}), f32[2,512,512]{2,0,1:T(2,128)}, u32[]{:S(2)}, u32[]{:S(2)}) async-start(f32[2,512,512]{2,0,1:T(2,128)} %copy.47), calls=%async_computation.1 | async-start | bytes 4194304 | tf_op jit(solution)/shard_map/all_to_all | solution.py:68
  82.5 0.0 all-gather.2.cloned.1.call-start
  82.5 0.0 copy-done.1
  82.5 0.0 copy-done.4
  82.5 1.4 fusion.7
  83.9 0.1 reduce_sum.62
  84.0 0.1 reduce_sum.63
  84.1 0.1 copy.58
  84.2 162.2 %psum.7 = f32[16,4]{0,1:T(4,128)S(1)} all-reduce(f32[16,4]{0,1:T(4,128)S(1)} %copy.58), channel_id=1, replica_groups=mesh['fsdp'=64,'group'=4] {'fsdp'}, use_global_device_ids=true, to_apply=%region_6.7 | all-reduce | flops 64 | bytes 512 | tf_op jit(solution)/shard_map/psum | solution.py:61
  246.4 0.1 select_reduce_fusion.1
  246.6 0.1 copy.50
  246.6 0.1 reshape.175
  246.7 0.8 gather_fusion.2
  247.5 0.1 add.108
  247.6 0.1 copy.51
  247.7 0.1 copy.52
  247.8 0.0 all-to-all-done.1
  247.8 3.3 %copy.48 = f32[2,512,512]{2,1,0:T(8,128)} copy(f32[2,512,512]{2,0,1:T(2,128)} %all-to-all-done.1) | data formatting | bytes 4194304 | tf_op jit(solution)/shard_map/all_to_all | solution.py:68
  251.1 2.2 gather_fusion.1
  253.3 0.9 multiply_convert_fusion
  254.3 0.0 all-gather.2.cloned.1.call-update
  254.3 2.1 multiply_bitcast_fusion.1
  256.4 0.0 copy-done.3
  256.4 2.0 multiply_bitcast_fusion
  258.4 24.2 %all-gather.2.cloned.1.call-done = bf16[16,8,8192]{2,1,0:T(8,128)(2,1)} async-done(((bf16[16,8,2048]{2,1,0:T(8,128)(2,1)}), bf16[16,8,8192]{2,1,0:T(8,128)(2,1)}) %all-gather.2.cloned.1.call-update) | async-done | bytes 2097168 | tf_op jit(solution)/shard_map/all_gather | solution.py:81
  282.6 3.1 %copy.64 = bf16[16,8,8192]{2,1,0:T(8,128)(2,1)} copy(bf16[16,8,8192]{2,1,0:T(8,128)(2,1)} %all-gather.2.cloned.1.call-done) | data formatting | bytes 4194304
  (9 shorter events, 0.1 us)
Async XLA Ops:
  7.2 49.0 %copy-start = (bf16[1,1,2,512,512]{4,3,2,1,0:T(8,128)(2,1)S(1)}, bf16[1,1,2,512,512]{4,3,2,1,0:T(8,128)(2,1)}, u32[]{:S(2)}) copy-start(bf16[1,1,2,512,512]{4,3,2,1,0:T(8,128)(2,1)} %param.10) | copy-start | bytes 3145732
  56.2 4.2 %copy-start.2 = (bf16[2,512,512]{1,2,0:T(8,128)(2,1)}, bf16[2,512,512]{1,2,0:T(8,128)(2,1)S(1)}, u32[]{:S(2)}) copy-start(bf16[2,512,512]{1,2,0:T(8,128)(2,1)S(1)} %copy.45) | copy-start | bytes 3145732
  61.1 15.4 %all-to-all-start.2 = ((f32[2,64,1]{0,2,1:T(1,128)}), f32[2,64,1]{0,2,1:T(1,128)S(1)}, u32[]{:S(2)}, u32[]{:S(2)}) async-start(f32[2,64,1]{0,2,1:T(1,128)} %broadcast_in_dim.76), calls=%async_computation.2 | async-start | bytes 65536 | tf_op jit(solution)/shard_map/all_to_all | solution.py:69
  71.8 10.7 %copy-start.1 = (bf16[16,8,2048]{2,1,0:T(8,128)(2,1)S(1)}, bf16[16,8,2048]{2,1,0:T(8,128)(2,1)}, u32[]{:S(2)}) copy-start(bf16[16,8,2048]{2,1,0:T(8,128)(2,1)} %param.7) | copy-start | bytes 1572868
  71.8 10.7 %copy-start.4 = (bf16[16,8,2048]{2,1,0:T(8,128)(2,1)S(1)}, bf16[16,8,2048]{2,1,0:T(8,128)(2,1)}, u32[]{:S(2)}) copy-start(bf16[16,8,2048]{2,1,0:T(8,128)(2,1)} %param.8) | copy-start | bytes 1572868
  76.5 171.3 %all-to-all-start.1 = ((f32[2,512,512]{2,0,1:T(2,128)}), f32[2,512,512]{2,0,1:T(2,128)}, u32[]{:S(2)}, u32[]{:S(2)}) async-start(f32[2,512,512]{2,0,1:T(2,128)} %copy.47), calls=%async_computation.1 | async-start | bytes 4194304 | tf_op jit(solution)/shard_map/all_to_all | solution.py:68
  82.5 200.2 %all-gather.2.cloned.1.call-start = ((), (), s32[]{:S(2)}) async-start(), calls=%async_computation.3 | async-start | bytes 2621440 | tf_op jit(solution)/shard_map/all_gather | solution.py:81
  254.3 2.1 copy-start.3
Sparse Core Ops, SparseCore 0:
  254.4 28.1 all-gather.1
where the time goes:
time: 293 us
  blocking collectives  204 us (70%)
  waiting for transfers between devices  28.9 us (10%)
  local copies, waits for them, and re-layouts  19.9 us (7%)
  between operations  14.2 us (5%)
  starting transfers between devices  12.2 us (4%)
  matrix products  8.31 us (3%)
  other arithmetic  5.48 us (2%)
    psum x1, blocking collectives, body(): adam_total = lax.psum(adam_partial, 'fsdp')  162 us
    all_to_all x1, blocking collectives, body(): lax.all_to_all(outgoing, 'fsdp', split_axis=1, concat_axis=1, tiled=True)  41.3 us
    all_gather x1, waiting for transfers between devices, body(): update = lax.all_gather(local_update, 'group', axis=2, tiled=True)  24.2 us
    all_to_all x1, starting transfers between devices, body(): lax.all_to_all(spread_mean, 'fsdp', split_axis=1, concat_axis=1, tiled=True)  6.19 us
    all_to_all x1, starting transfers between devices, body(): lax.all_to_all(precond, 'fsdp', split_axis=1, concat_axis=1, tiled=True)  5.98 us
  transfers between devices with their start and end apart: 3, of which 2 were waited for; matrix products, arithmetic and copies ran while one was open for 4% of the time, Pallas kernels for 0%

commit v1 on v0

v1 whole, which is shorter than its diff:
```python
import functools

import jax
import jax.numpy as jnp
from jax import lax
from jax.experimental import pallas as pl
from jax.experimental.pallas import tpu as pltpu
from jax.sharding import PartitionSpec as P

MESH = pl.DeviceIdType.MESH
F32 = jnp.float32
BF16 = jnp.bfloat16

N = 64
X, Z, C = 4, 8, 2
Q = 4
T = 512
BANDS = 16
R = 8
W = 2048
NC = W // T
IN_CHUNKS = 2
OUT_CHUNKS = 4
IW = T // IN_CHUNKS
OW = T // OUT_CHUNKS


def peer(me, k):
    step = k // 8
    half = (step + 1) // 2
    far = jnp.where(step % 2 == 1, half, Z - half)
    dz = lax.rem(4 + far, Z)
    dx = (k // 2 + 2) % X
    dc = k % 2
    c = lax.rem(me, C)
    z = lax.rem(lax.div(me, C), Z)
    x = lax.div(me, C * Z)
    return (lax.rem(x + dx, X) * Z + lax.rem(z + dz, Z)) * C + lax.rem(c + dc, C)


def others(me, fn):
    def one(k, carry):
        d = peer(me, k)
        fn(d)
        return carry

    own = SELF
    lax.fori_loop(0, own, one, 0)
    lax.fori_loop(own + 1, N, one, 0)


def find_self():
    for k in range(N):
        step = k // 8
        half = (step + 1) // 2
        far = half if step % 2 == 1 else Z - half
        if (4 + far) % Z == 0 and (k // 2 + 2) % X == 0 and k % 2 == 0:
            return k


SELF = find_self()


def exchange_kernel(
    idx, g_hbm, m_hbm, l_hbm, r_hbm, y_out, g_out,
    gv, mv, lv, rv, pieces, apart, send_g, recv_g, grad, pre, send_u, ru0, ru1, ru2, ru3, ysrc, send_a, recv_a,
    load_sem, gs, gr, as_, ar, us, ur, ys, yr, keep_sem,
):
    recv_u = (ru0, ru1, ru2, ru3)
    me = lax.axis_index("fsdp")
    mine = lax.axis_index("group")

    barrier = pltpu.get_barrier_semaphore()
    others(me, lambda d: pl.semaphore_signal(barrier, inc=1, device_id={"fsdp": d}, device_id_type=MESH))
    for k in range(1, Q):
        pl.semaphore_signal(
            barrier, inc=1, device_id={"group": lax.rem(mine + k, Q)}, device_id_type=MESH
        )

    loads = [
        pltpu.make_async_copy(src, dst, load_sem.at[i])
        for i, (src, dst) in enumerate([(g_hbm, gv), (m_hbm, mv), (l_hbm, lv), (r_hbm, rv)])
    ]
    for load in loads:
        load.start()
    loads[0].wait()

    def split(b, carry):
        rows = gv[b].astype(F32)
        for c in range(NC):
            pieces[b * NC + c] = rows[:, c * T : (c + 1) * T]
        return carry

    lax.fori_loop(0, BANDS, split, 0)
    pieces[N] = jnp.zeros((R, T), F32)

    def pack(o, carry):
        both = jnp.concatenate([pieces[idx[0, o]], pieces[idx[1, o]]], axis=0)
        send_g[o] = both.astype(BF16)
        return carry

    lax.fori_loop(0, N, pack, 0)

    pl.semaphore_wait(barrier, N - 1 + Q - 1)

    for j in range(IN_CHUNKS):
        cols = pl.ds(j * IW, IW)

        def send(d, cols=cols, j=j):
            pltpu.make_async_remote_copy(
                send_g.at[d, :, cols], recv_g.at[me, :, cols], gs.at[j], gr.at[j],
                device_id={"fsdp": d}, device_id_type=MESH,
            ).start()

        others(me, send)
    recv_g[me] = send_g[me]

    loads[1].wait()

    def adam(b, carry):
        g = gv[b].astype(F32)
        m = mv[b].astype(F32)
        moment = (0.95 * m + 0.05 * g * g).astype(BF16).astype(F32)
        a = g / (jnp.sqrt(moment) + 1e-8)
        sq = a * a
        for c in range(NC):
            part = sq[:, c * T : c * T + 128]
            for i in range(1, T // 128):
                part = part + sq[:, c * T + i * 128 : c * T + (i + 1) * 128]
            apart[b * NC + c] = part
        return carry

    lax.fori_loop(0, BANDS, adam, 0)
    apart[N] = jnp.zeros((R, 128), F32)

    def pack_adam(o, carry):
        first = jnp.sum(apart[idx[0, o]], axis=0, keepdims=True)
        second = jnp.sum(apart[idx[1, o]], axis=0, keepdims=True)
        send_a[o] = jnp.concatenate([first, second], axis=0)
        return carry

    lax.fori_loop(0, N, pack_adam, 0)

    def send_adam(d):
        pltpu.make_async_remote_copy(
            send_a.at[d], recv_a.at[me], as_, ar, device_id={"fsdp": d}, device_id_type=MESH
        ).start()

    others(me, send_adam)
    recv_a[me] = send_a[me]

    loads[2].wait()
    loads[3].wait()

    group_rows = 8
    for j in range(IN_CHUNKS):
        cols = pl.ds(j * IW, IW)
        got = recv_g.at[pl.ds(0, N - 1), :, cols]
        pltpu.make_async_copy(got, got, gr.at[j]).wait()

        def sort(t, carry, cols=cols):
            v = recv_g[pl.ds(t * group_rows, group_rows), :, cols].astype(F32)
            for s in range(2):
                rows = v[:, s * R : (s + 1) * R, :].reshape(group_rows * R, IW)
                grad[s, pl.ds(t * group_rows * R, group_rows * R), cols] = rows.astype(BF16)
            return carry

        lax.fori_loop(0, N // group_rows, sort, 0)
        for s in range(2):
            half = jnp.dot(lv[s], grad[s, :, cols], preferred_element_type=F32).astype(BF16)
            out = jnp.dot(half, rv[s, cols, :], preferred_element_type=F32)
            if j == 0:
                pre[s] = out
            else:
                pre[s] = pre[s] + out

    keep = pltpu.make_async_copy(grad, g_out, keep_sem.at[0])
    keep.start()

    got = recv_a.at[pl.ds(0, N - 1)]
    pltpu.make_async_copy(got, got, ar).wait()
    a_sum = jnp.sum(jnp.sum(recv_a[...], axis=0), axis=1, keepdims=True)
    scale = []
    for s in range(2):
        sq = jnp.sum(pre[s] * pre[s], axis=0, keepdims=True)
        p_mean = jnp.sum(sq, axis=1, keepdims=True) / (T * T)
        scale.append(jnp.sqrt(a_sum[s : s + 1] / (T * T) / (p_mean + 1e-6)))

    for j in range(OUT_CHUNKS):
        cols = pl.ds(j * OW, OW)
        tiles = [(pre[s, :, cols] * scale[s]).reshape(N, R, OW) for s in range(2)]
        send_u[j] = jnp.concatenate(tiles, axis=1).astype(BF16)

        def send(d, j=j):
            pltpu.make_async_remote_copy(
                send_u.at[j, d], recv_u[j].at[me], us.at[j], ur.at[j],
                device_id={"fsdp": d}, device_id_type=MESH,
            ).start()

        others(me, send)
        recv_u[j][me] = send_u[j, me]

    gathers = []
    for j in range(OUT_CHUNKS):
        got = recv_u[j].at[pl.ds(0, N - 1)]
        pltpu.make_async_copy(got, got, ur.at[j]).wait()

        def pick(bp, carry, j=j):
            for c in range(NC):
                rows = []
                for e in range(2):
                    p = (2 * bp + e) * NC + c
                    t = recv_u[j][idx[2, p]].astype(F32)
                    rows.append(jnp.where(idx[3, p] == 0, t[:R], t[R:]))
                ysrc[j, pl.ds(bp * 2 * R, 2 * R), c * OW : (c + 1) * OW] = jnp.concatenate(
                    rows, axis=0
                ).astype(BF16)
            return carry

        lax.fori_loop(0, BANDS // 2, pick, 0)
        for k in (2, 1, 3):
            copy = pltpu.make_async_remote_copy(
                ysrc.at[j], y_out.at[mine, j], ys.at[j, k - 1], yr.at[j, k - 1],
                device_id={"group": lax.rem(mine + k, Q)}, device_id_type=MESH,
            )
            copy.start()
            gathers.append(copy)
        local = pltpu.make_async_copy(ysrc.at[j], y_out.at[mine, j], keep_sem.at[1 + j])
        local.start()
        gathers.append(local)

    keep.wait()
    for copy in gathers:
        copy.wait()
    for j in range(IN_CHUNKS):
        sent = send_g.at[pl.ds(0, N - 1), :, pl.ds(j * IW, IW)]
        pltpu.make_async_copy(sent, sent, gs.at[j]).wait()
    for j in range(OUT_CHUNKS):
        sent = send_u.at[j, pl.ds(0, N - 1)]
        pltpu.make_async_copy(sent, sent, us.at[j]).wait()
    sent = send_a.at[pl.ds(0, N - 1)]
    pltpu.make_async_copy(sent, sent, as_).wait()


def finish_kernel(y, g, m, gr, update, moment, left, right):
    for j in range(OUT_CHUNKS):
        for c in range(NC):
            tile = y[0, j, :, c * OW : (c + 1) * OW].astype(F32).reshape(BANDS, R, OW)
            update[:, :, c * T + j * OW : c * T + (j + 1) * OW] = tile.astype(BF16)
    wide = g[...].astype(F32)
    moment[...] = (0.95 * m[...].astype(F32) + 0.05 * wide * wide).astype(BF16)
    h = lax.rem(pl.program_id(0), 2) * 256
    part = pl.ds(pl.multiple_of(h, 256), 256)
    whole = gr[0]
    left[0, 0, 0] = (
        lax.dot_general(gr[0, part, :], whole, (((1,), (1,)), ((), ())), preferred_element_type=F32) / T
    )
    right[0, 0, 0] = (
        lax.dot_general(gr[0, :, part], whole, (((0,), (0,)), ((), ())), preferred_element_type=F32) / T
    )


def positions(block_owner, row_offset, col_offset):
    col = col_offset // T
    piece = (row_offset // T) * NC + col % NC
    here = (col // NC) == lax.axis_index("group")
    code = jnp.arange(block_owner.shape[0], dtype=jnp.int32) * N + piece
    ids = jnp.arange(N, dtype=jnp.int32)
    match = (block_owner[None, :] == ids[:, None]) & here[None, :]
    first = jnp.min(jnp.where(match, code[None, :], 1 << 20), axis=1)
    last = jnp.max(jnp.where(match, code[None, :], -1), axis=1)
    p0 = jnp.where(last >= 0, first % N, N)
    p1 = jnp.where(last > first, last % N, N)
    is0 = p0[None, :] == ids[:, None]
    is1 = p1[None, :] == ids[:, None]
    owner = jnp.sum(jnp.where(is0 | is1, ids[None, :], 0), axis=1)
    slot = jnp.sum(is1.astype(jnp.int32), axis=1)
    return jnp.stack([p0, p1, owner, slot])


def body(gradient, second_moment, left_root, right_root, block_owner, row_offset, col_offset):
    idx = positions(block_owner, row_offset, col_offset)
    hbm = pl.BlockSpec(memory_space=pl.ANY)
    dma = pltpu.SemaphoreType.DMA
    y_all, grad = pl.pallas_call(
        exchange_kernel,
        out_shape=[
            jax.ShapeDtypeStruct((Q, OUT_CHUNKS, BANDS * R, NC * OW), BF16),
            jax.ShapeDtypeStruct((2, T, T), BF16),
        ],
        in_specs=[pl.BlockSpec(memory_space=pltpu.SMEM), hbm, hbm, hbm, hbm],
        out_specs=[hbm, hbm],
        scratch_shapes=[
            pltpu.VMEM((BANDS, R, W), BF16),
            pltpu.VMEM((BANDS, R, W), BF16),
            pltpu.VMEM((2, T, T), BF16),
            pltpu.VMEM((2, T, T), BF16),
            pltpu.VMEM((N + 1, R, T), F32),
            pltpu.VMEM((N + 1, R, 128), F32),
            pltpu.VMEM((N, 2 * R, T), BF16),
            pltpu.VMEM((N, 2 * R, T), BF16),
            pltpu.VMEM((2, T, T), BF16),
            pltpu.VMEM((2, T, T), F32),
            pltpu.VMEM((OUT_CHUNKS, N, 2 * R, OW), BF16),
            *[pltpu.VMEM((N, 2 * R, OW), BF16)] * OUT_CHUNKS,
            pltpu.VMEM((OUT_CHUNKS, BANDS * R, NC * OW), BF16),
            pltpu.VMEM((N, 2, 128), F32),
            pltpu.VMEM((N, 2, 128), F32),
            dma((4,)),
            dma((IN_CHUNKS,)),
            dma((IN_CHUNKS,)),
            dma,
            dma,
            dma((OUT_CHUNKS,)),
            dma((OUT_CHUNKS,)),
            dma((OUT_CHUNKS, Q - 1)),
            dma((OUT_CHUNKS, Q - 1)),
            dma((1 + OUT_CHUNKS,)),
        ],
        compiler_params=pltpu.CompilerParams(
            collective_id=0, has_side_effects=True, vmem_limit_bytes=60 << 20
        ),
    )(idx, gradient, second_moment, left_root[0, 0], right_root[0, 0])

    steps = 4
    stat = pl.BlockSpec((1, 1, 1, T // 2, T), lambda t: (0, 0, t // 2, t % 2, 0))
    bands = pl.BlockSpec((BANDS // steps, R, W), lambda t: (t, 0, 0))
    update, moment, left, right = pl.pallas_call(
        finish_kernel,
        grid=(steps,),
        out_shape=[
            jax.ShapeDtypeStruct((BANDS, R, Q * W), BF16),
            jax.ShapeDtypeStruct((BANDS, R, W), BF16),
            jax.ShapeDtypeStruct((1, 1, 2, T, T), F32),
            jax.ShapeDtypeStruct((1, 1, 2, T, T), F32),
        ],
        in_specs=[
            pl.BlockSpec((1, OUT_CHUNKS, BANDS * R, NC * OW), lambda t: (t, 0, 0, 0)),
            bands,
            bands,
            pl.BlockSpec((1, T, T), lambda t: (t // 2, 0, 0)),
        ],
        out_specs=[pl.BlockSpec((BANDS, R, W), lambda t: (0, 0, t)), bands, stat, stat],
        compiler_params=pltpu.CompilerParams(vmem_limit_bytes=60 << 20),
    )(y_all, gradient, second_moment, grad)
    return update, moment, left, right


def solution(mesh):
    placed = P(None, "fsdp", "group")
    slots = P("fsdp", "group", None, None, None)
    return jax.shard_map(
        body,
        mesh=mesh,
        in_specs=(placed, placed, slots, slots, P(), P(), P()),
        out_specs=(P(None, "fsdp", None), placed, slots, slots),
        check_vma=False,
    )
```

time: 293 us -> 88.6 us (0.30)
  blocking collectives: 204 us -> 0 us
  Pallas kernels: 0 us -> 84.7 us
  waiting for transfers between devices: 28.9 us -> 0 us
  local copies, waits for them, and re-layouts: 19.9 us -> 0 us
  between operations: 14.2 us -> 0.67 us
  starting transfers between devices: 12.2 us -> 0 us
  matrix products: 8.31 us -> 0 us
    psum x1 -> x0, blocking collectives: 162 us -> none  [body(): adam_total = lax.psum(adam_partial, 'fsdp')]
    pallas_call x0 -> x2, Pallas kernels: none -> 84.7 us  [the longest x1 77.9 us: body(): pl.pallas_call(exchange_kernel, out_shape=[jax.ShapeDtypeStruct((Q, OUT_C...]
    all_to_all x1 -> x0, blocking collectives: 41.3 us -> none  [body(): lax.all_to_all(outgoing, 'fsdp', split_axis=1, concat_axis=1, tiled=True)]
    all_gather x1 -> x0, waiting for transfers between devices: 24.2 us -> none  [body(): update = lax.all_gather(local_update, 'group', axis=2, tiled=True)]
    all_to_all x2 -> x0, starting transfers between devices: 12.2 us -> none  [the longest x1 6.19 us: body(): lax.all_to_all(spread_mean, 'fsdp', split_axis=1, concat_axis=1, tiled=True)]
    dot_general x3 -> x0, matrix products: 8.31 us -> none  [the longest x1 4.21 us: body(): jnp.einsum('sij,sjk->sik', half_done, right_root[0, 0], preferred_element...]
    gather x3 -> x0, local copies, waits for them, and re-layouts: 4.89 us -> none  [the longest x1 2.2 us: body(): picked = returned[key_of_piece]]
    all_to_all x3 -> x0, local copies, waits for them, and re-layouts: 4.85 us -> none  [the longest x1 3.34 us: body(): lax.all_to_all(precond, 'fsdp', split_axis=1, concat_axis=1, tiled=True)]
  transfers between devices with their start and end apart: 3 -> 0, of which waited for: 2 -> 0; matrix products, arithmetic and copies ran while one was open for 4% -> 0% of each run, Pallas kernels for 0% -> 0%
where the time goes in v1:
time: 88.6 us; the launch traced here: 88.3 us
  Pallas kernels  84.7 us (96%)
  other arithmetic  2.93 us (3%)
    pallas_call x1, Pallas kernels, body(): pl.pallas_call(exchange_kernel, out_shape=[jax.ShapeDtypeStruct((Q, OUT_C...  77.9 us
    pallas_call x1, Pallas kernels, body(): pl.pallas_call(finish_kernel, grid=(steps,), out_shape=[jax.ShapeDtypeStr...  6.86 us

profile of v1, /device:TPU:1, one launch (start us, length us, event | category | flops | bytes accessed | tf_op | source)
XLA Modules:
  0.0 88.3 jit_solution(5106961677142221668)
XLA Ops:
  0.6 0.7 fusion.4
  1.3 0.7 fusion.3
  2.0 0.8 select_reduce_fusion
  2.9 0.1 select_reduce_fusion.2
  3.0 0.6 pad_add_fusion.idx
  3.6 77.9 %shard_map.102 = (bf16[4,4,128,512]{3,2,1,0:T(8,128)(2,1)}, bf16[2,512,512]{2,1,0:T(8,128)(2,1)}) custom-call(s32[4,64]{1,0:T(4,128)} %pad_add_fusion.idx, bf16[16,8,2048]{2,1,0:T(8,128)(2,1)} %g.1, bf16[16,8,2048]{2,1,0:T(8,128)(2,1)} %m.1, bf16[2,512,512]{2,1,0:T(8,128)(2,1)} %bitcast.10, bf16[2,512,512]{2,1,0:T(8,128)(2,1)} %bitcast.11), custom_call_target="tpu_custom_call" | custom-call | tf_op jit(solution)/shard_map/pallas_call | solution.py:285
  81.5 6.9 %shard_map.103 = (bf16[16,8,8192]{2,1,0:T(8,128)(2,1)}, bf16[16,8,2048]{2,1,0:T(8,128)(2,1)}, f32[1,1,2,512,512]{4,3,2,1,0:T(8,128)}, f32[1,1,2,512,512]{4,3,2,1,0:T(8,128)}) custom-call(bf16[4,4,128,512]{3,2,1,0:T(8,128)(2,1)} %get-tuple-element.6.y, bf16[16,8,2048]{2,1,0:T(8,128)(2,1)} %g.1, bf16[16,8,2048]{2,1,0:T(8,128)(2,1)} %m.1, ...), custom_call_target="tpu_custom_call" | custom-call | tf_op jit(solution)/shard_map/pallas_call | solution.py:328
  (2 shorter events, 0.0 us)

commit v2 on v1

v2 whole, which is shorter than its diff:
```python
import functools

import jax
import jax.numpy as jnp
from jax import lax
from jax.experimental import pallas as pl
from jax.experimental.pallas import tpu as pltpu
from jax.sharding import PartitionSpec as P

MESH = pl.DeviceIdType.MESH
F32 = jnp.float32
BF16 = jnp.bfloat16

N = 64
X, Z, C = 4, 8, 2
Q = 4
T = 512
BANDS = 16
R = 8
W = 2048
NC = W // T
IN_CHUNKS = 2
OUT_CHUNKS = 4
IW = T // IN_CHUNKS
OW = T // OUT_CHUNKS


def peer(me, k):
    step = k // 8
    half = (step + 1) // 2
    far = jnp.where(step % 2 == 1, half, Z - half)
    dz = lax.rem(4 + far, Z)
    dx = (k // 2 + 2) % X
    dc = k % 2
    c = lax.rem(me, C)
    z = lax.rem(lax.div(me, C), Z)
    x = lax.div(me, C * Z)
    return (lax.rem(x + dx, X) * Z + lax.rem(z + dz, Z)) * C + lax.rem(c + dc, C)


def others(me, fn):
    def one(k, carry):
        d = peer(me, k)
        fn(d)
        return carry

    own = SELF
    lax.fori_loop(0, own, one, 0)
    lax.fori_loop(own + 1, N, one, 0)


def find_self():
    for k in range(N):
        step = k // 8
        half = (step + 1) // 2
        far = half if step % 2 == 1 else Z - half
        if (4 + far) % Z == 0 and (k // 2 + 2) % X == 0 and k % 2 == 0:
            return k


SELF = find_self()


def exchange_kernel(
    o_hbm, r0_hbm, c0_hbm, g_hbm, m_hbm, l_hbm, r_hbm, y_all, moment, left, right,
    where_v, idx_v, idx, gv, mv, lv, rv, pieces, apart, send_g, recv_g, grad, pre,
    send_u, ru0, ru1, ru2, ru3, send_a, recv_a,
    load_sem, idx_sem, gs, gr, as_, ar, us, ur, ys, yr,
):
    recv_u = (ru0, ru1, ru2, ru3)
    me = lax.axis_index("fsdp")
    mine = lax.axis_index("group")

    loads = [
        pltpu.make_async_copy(src, dst, load_sem.at[i])
        for i, (src, dst) in enumerate(
            [
                (g_hbm, gv), (m_hbm, mv), (l_hbm, lv), (r_hbm, rv),
                (o_hbm, where_v.at[0]), (r0_hbm, where_v.at[1]), (c0_hbm, where_v.at[2]),
            ]
        )
    ]
    for i in (4, 5, 6, 0, 1, 2, 3):
        loads[i].start()

    barrier = pltpu.get_barrier_semaphore()
    others(me, lambda d: pl.semaphore_signal(barrier, inc=1, device_id={"fsdp": d}, device_id_type=MESH))
    for k in range(1, Q):
        pl.semaphore_signal(
            barrier, inc=1, device_id={"group": lax.rem(mine + k, Q)}, device_id_type=MESH
        )

    for i in (4, 5, 6):
        loads[i].wait()
    positions(where_v, idx_v, mine)
    to_smem = pltpu.make_async_copy(idx_v, idx, idx_sem)
    to_smem.start()

    loads[0].wait()

    def split(b, carry):
        rows = gv[b].astype(F32)
        for c in range(NC):
            pieces[b * NC + c] = rows[:, c * T : (c + 1) * T]
        return carry

    lax.fori_loop(0, BANDS, split, 0)
    pieces[N] = jnp.zeros((R, T), F32)
    to_smem.wait()

    def pack(o, carry):
        both = jnp.concatenate([pieces[idx[0, o]], pieces[idx[1, o]]], axis=0)
        send_g[o] = both.astype(BF16)
        return carry

    lax.fori_loop(0, N, pack, 0)

    pl.semaphore_wait(barrier, N - 1 + Q - 1)

    def send_chunk(j):
        cols = pl.ds(j * IW, IW)

        def send(d):
            pltpu.make_async_remote_copy(
                send_g.at[d, :, cols], recv_g.at[me, :, cols], gs.at[j], gr.at[j],
                device_id={"fsdp": d}, device_id_type=MESH,
            ).start()

        others(me, send)

    send_chunk(0)
    recv_g[me] = send_g[me]

    loads[1].wait()

    def adam(b, carry):
        g = gv[b].astype(F32)
        m = mv[b].astype(F32)
        second = (0.95 * m + 0.05 * g * g).astype(BF16)
        moment[b] = second
        a = g / (jnp.sqrt(second.astype(F32)) + 1e-8)
        sq = a * a
        for c in range(NC):
            part = sq[:, c * T : c * T + 128]
            for i in range(1, T // 128):
                part = part + sq[:, c * T + i * 128 : c * T + (i + 1) * 128]
            apart[b * NC + c] = part
        return carry

    lax.fori_loop(0, BANDS, adam, 0)
    apart[N] = jnp.zeros((R, 128), F32)

    def pack_adam(o, carry):
        first = jnp.sum(apart[idx[0, o]], axis=0, keepdims=True)
        second = jnp.sum(apart[idx[1, o]], axis=0, keepdims=True)
        send_a[o] = jnp.concatenate([first, second], axis=0)
        return carry

    lax.fori_loop(0, N, pack_adam, 0)

    def send_adam(d):
        pltpu.make_async_remote_copy(
            send_a.at[d], recv_a.at[me], as_, ar, device_id={"fsdp": d}, device_id_type=MESH
        ).start()

    others(me, send_adam)
    for j in range(1, IN_CHUNKS):
        send_chunk(j)
    recv_a[me] = send_a[me]

    loads[2].wait()
    loads[3].wait()

    group_rows = 8
    for j in range(IN_CHUNKS):
        cols = pl.ds(j * IW, IW)
        got = recv_g.at[pl.ds(0, N - 1), :, cols]
        pltpu.make_async_copy(got, got, gr.at[j]).wait()

        def sort(t, carry, cols=cols):
            v = recv_g[pl.ds(t * group_rows, group_rows), :, cols].astype(F32)
            for s in range(2):
                rows = v[:, s * R : (s + 1) * R, :].reshape(group_rows * R, IW)
                grad[s, pl.ds(t * group_rows * R, group_rows * R), cols] = rows.astype(BF16)
            return carry

        lax.fori_loop(0, N // group_rows, sort, 0)
        for s in range(2):
            half = jnp.dot(lv[s], grad[s, :, cols], preferred_element_type=F32).astype(BF16)
            out = jnp.dot(half, rv[s, cols, :], preferred_element_type=F32)
            if j == 0:
                pre[s] = out
            else:
                pre[s] = pre[s] + out

    got = recv_a.at[pl.ds(0, N - 1)]
    pltpu.make_async_copy(got, got, ar).wait()
    a_sum = jnp.sum(jnp.sum(recv_a[...], axis=0), axis=1, keepdims=True)
    scale = []
    for s in range(2):
        sq = jnp.sum(pre[s] * pre[s], axis=0, keepdims=True)
        p_mean = jnp.sum(sq, axis=1, keepdims=True) / (T * T)
        scale.append(jnp.sqrt(a_sum[s : s + 1] / (T * T) / (p_mean + 1e-6)))

    for j in range(OUT_CHUNKS):
        cols = pl.ds(j * OW, OW)
        tiles = [(pre[s, :, cols] * scale[s]).reshape(N, R, OW) for s in range(2)]
        send_u[j] = jnp.concatenate(tiles, axis=1).astype(BF16)

        def send(d, j=j):
            pltpu.make_async_remote_copy(
                send_u.at[j, d], recv_u[j].at[me], us.at[j], ur.at[j],
                device_id={"fsdp": d}, device_id_type=MESH,
            ).start()

        others(me, send)
        recv_u[j][me] = send_u[j, me]

    for s in range(2):
        g = grad[s]
        left[s] = (
            lax.dot_general(g, g, (((1,), (1,)), ((), ())), preferred_element_type=F32) / T
        )
        right[s] = (
            lax.dot_general(g, g, (((0,), (0,)), ((), ())), preferred_element_type=F32) / T
        )

    gathers = []
    for j in range(OUT_CHUNKS):
        got = recv_u[j].at[pl.ds(0, N - 1)]
        pltpu.make_async_copy(got, got, ur.at[j]).wait()

        def pick(b, carry, j=j):
            for c in range(NC):
                p = b * NC + c
                t = recv_u[j][idx[2, p]].astype(F32)
                rows = jnp.where(idx[3, p] == 0, t[:R], t[R:])
                y_all[mine, j, b, :, c * OW : (c + 1) * OW] = rows.astype(BF16)
            return carry

        lax.fori_loop(0, BANDS, pick, 0)
        for k in (2, 1, 3):
            copy = pltpu.make_async_remote_copy(
                y_all.at[mine, j], y_all.at[mine, j], ys.at[j, k - 1], yr.at[j, k - 1],
                device_id={"group": lax.rem(mine + k, Q)}, device_id_type=MESH,
            )
            copy.start()
            gathers.append(copy)

    for copy in gathers:
        copy.wait()
    for j in range(IN_CHUNKS):
        sent = send_g.at[pl.ds(0, N - 1), :, pl.ds(j * IW, IW)]
        pltpu.make_async_copy(sent, sent, gs.at[j]).wait()
    for j in range(OUT_CHUNKS):
        sent = send_u.at[j, pl.ds(0, N - 1)]
        pltpu.make_async_copy(sent, sent, us.at[j]).wait()
    sent = send_a.at[pl.ds(0, N - 1)]
    pltpu.make_async_copy(sent, sent, as_).wait()


def finish_kernel(y_all, moment, left, right, update_out, moment_out, left_out, right_out, sem):
    copies = [
        pltpu.make_async_copy(left, left_out.at[0, 0], sem.at[0]),
        pltpu.make_async_copy(right, right_out.at[0, 0], sem.at[1]),
        pltpu.make_async_copy(moment, moment_out, sem.at[2]),
    ]
    for q in range(Q):
        for j in range(OUT_CHUNKS):
            for c in range(NC):
                copies.append(
                    pltpu.make_async_copy(
                        y_all.at[q, j, :, :, pl.ds(c * OW, OW)],
                        update_out.at[:, :, pl.ds(q * W + c * T + j * OW, OW)],
                        sem.at[len(copies)],
                    )
                )
    for copy in copies:
        copy.start()
    for copy in copies:
        copy.wait()


def positions(where_v, out, mine):
    owner, row, col = where_v[0], where_v[1], where_v[2]
    blocks = owner.shape[1]
    col = col // T
    piece = (row // T) * NC + col % NC
    here = (col // NC) == mine
    code = lax.broadcasted_iota(jnp.int32, (1, blocks), 1) * N + piece
    owner = jnp.where(here, owner, N)
    match = owner == lax.broadcasted_iota(jnp.int32, (N, blocks), 0)
    first = jnp.min(jnp.where(match, code, 1 << 20), axis=1, keepdims=True)
    last = jnp.max(jnp.where(match, code, -1), axis=1, keepdims=True)
    p0 = jnp.where(last >= 0, first % N, N)
    p1 = jnp.where(last > first, last % N, N)
    sub = lax.broadcasted_iota(jnp.int32, (N, 128), 0)
    lane = lax.broadcasted_iota(jnp.int32, (N, 128), 1)
    own_lane = sub == lane
    is0, is1 = p0 == lane, p1 == lane

    def total(v):
        return jnp.sum(v, axis=0, keepdims=True)

    out[0:1] = total(jnp.where(own_lane, p0, 0))
    out[1:2] = total(jnp.where(own_lane, p1, 0))
    out[2:3] = total(jnp.where(is0 | is1, sub, 0))
    out[3:4] = total(jnp.where(is1, 1, 0))


def body(gradient, second_moment, left_root, right_root, block_owner, row_offset, col_offset):
    hbm = pl.BlockSpec(memory_space=pltpu.HBM)
    vmem = pl.BlockSpec(memory_space=pltpu.VMEM)
    dma = pltpu.SemaphoreType.DMA
    blocks = block_owner.shape[0]
    places = [v.reshape(1, blocks) for v in (block_owner, row_offset, col_offset)]
    operands = [
        pltpu.with_memory_space_constraint(v, pltpu.HBM)
        for v in (*places, gradient, second_moment, left_root[0, 0], right_root[0, 0])
    ]
    kept = pl.pallas_call(
        exchange_kernel,
        out_shape=[
            pltpu.VMEM((Q, OUT_CHUNKS, BANDS, R, NC * OW), BF16),
            pltpu.VMEM((BANDS, R, W), BF16),
            pltpu.VMEM((2, T, T), F32),
            pltpu.VMEM((2, T, T), F32),
        ],
        in_specs=[hbm] * 7,
        out_specs=[vmem] * 4,
        scratch_shapes=[
            pltpu.VMEM((3, 1, blocks), jnp.int32),
            pltpu.VMEM((8, 128), jnp.int32),
            pltpu.SMEM((8, 128), jnp.int32),
            pltpu.VMEM((BANDS, R, W), BF16),
            pltpu.VMEM((BANDS, R, W), BF16),
            pltpu.VMEM((2, T, T), BF16),
            pltpu.VMEM((2, T, T), BF16),
            pltpu.VMEM((N + 1, R, T), F32),
            pltpu.VMEM((N + 1, R, 128), F32),
            pltpu.VMEM((N, 2 * R, T), BF16),
            pltpu.VMEM((N, 2 * R, T), BF16),
            pltpu.VMEM((2, T, T), BF16),
            pltpu.VMEM((2, T, T), F32),
            pltpu.VMEM((OUT_CHUNKS, N, 2 * R, OW), BF16),
            *[pltpu.VMEM((N, 2 * R, OW), BF16)] * OUT_CHUNKS,
            pltpu.VMEM((N, 2, 128), F32),
            pltpu.VMEM((N, 2, 128), F32),
            dma((7,)),
            dma,
            dma((IN_CHUNKS,)),
            dma((IN_CHUNKS,)),
            dma,
            dma,
            dma((OUT_CHUNKS,)),
            dma((OUT_CHUNKS,)),
            dma((OUT_CHUNKS, Q - 1)),
            dma((OUT_CHUNKS, Q - 1)),
        ],
        compiler_params=pltpu.CompilerParams(
            collective_id=0, has_side_effects=True, vmem_limit_bytes=32 << 20
        ),
    )(*operands)

    return pl.pallas_call(
        finish_kernel,
        out_shape=[
            jax.ShapeDtypeStruct((BANDS, R, Q * W), BF16),
            jax.ShapeDtypeStruct((BANDS, R, W), BF16),
            jax.ShapeDtypeStruct((1, 1, 2, T, T), F32),
            jax.ShapeDtypeStruct((1, 1, 2, T, T), F32),
        ],
        in_specs=[vmem] * 4,
        out_specs=[hbm] * 4,
        scratch_shapes=[dma((3 + Q * OUT_CHUNKS * NC,))],
        compiler_params=pltpu.CompilerParams(vmem_limit_bytes=16 << 20),
    )(*kept)


def solution(mesh):
    placed = P(None, "fsdp", "group")
    slots = P("fsdp", "group", None, None, None)
    return jax.shard_map(
        body,
        mesh=mesh,
        in_specs=(placed, placed, slots, slots, P(), P(), P()),
        out_specs=(P(None, "fsdp", None), placed, slots, slots),
        check_vma=False,
    )
```

time: 88.6 us -> 82 us (0.926)
  Pallas kernels: 84.7 us -> 81.3 us
  other arithmetic: 2.93 us -> 0 us
    pallas_call x2, Pallas kernels: 84.7 us -> 81.3 us  [the longest x1 77.9 us: body(): pl.pallas_call(exchange_kernel, out_shape=[pltpu.VMEM((Q, OUT_CHUNKS, BAN...]
where the time goes in v2:
time: 82 us; the launch traced here: 81.9 us
  Pallas kernels  81.3 us (99%)
    pallas_call x1, Pallas kernels, body(): pl.pallas_call(exchange_kernel, out_shape=[pltpu.VMEM((Q, OUT_CHUNKS, BAN...  77.9 us
    pallas_call x1, Pallas kernels, body(): pl.pallas_call(finish_kernel, out_shape=[jax.ShapeDtypeStruct((BANDS, R,...  3.35 us

profile of v2, /device:TPU:1, one launch (start us, length us, event | category | flops | bytes accessed | tf_op | source)
XLA Modules:
  0.0 81.9 jit_solution(2578834988968339764)
XLA Ops:
  0.6 77.9 %shard_map.102 = (bf16[4,4,16,8,512]{4,3,2,1,0:T(8,128)(2,1)S(1)}, bf16[16,8,2048]{2,1,0:T(8,128)(2,1)S(1)}, f32[2,512,512]{2,1,0:T(8,128)S(1)}, f32[2,512,512]{2,1,0:T(8,128)S(1)}) custom-call(s32[1,256]{1,0:T(1,128)} %bitcast.7, s32[1,256]{1,0:T(1,128)} %bitcast.8, s32[1,256]{1,0:T(1,128)} %bitcast.9, bf16[16,8,2048]{2,1,0:T(8,128)(2,1)} %g_hbm.1, ...), custom_call_target="tpu_custom_call" | custom-call | tf_op jit(solution)/shard_map/pallas_call | solution.py:321
  78.6 3.4 %shard_map.103 = (bf16[16,8,8192]{2,1,0:T(8,128)(2,1)}, bf16[16,8,2048]{2,1,0:T(8,128)(2,1)}, f32[1,1,2,512,512]{4,3,2,1,0:T(8,128)}, f32[1,1,2,512,512]{4,3,2,1,0:T(8,128)}) custom-call(bf16[4,4,16,8,512]{4,3,2,1,0:T(8,128)(2,1)S(1)} %get-tuple-element.8.y_all, bf16[16,8,2048]{2,1,0:T(8,128)(2,1)S(1)} %get-tuple-element.9.moment, ...), custom_call_target="tpu_custom_call" | custom-call | tf_op jit(solution)/shard_map/pallas_call | solution.py:365

commit v3 on v2

--- a/solution.py
+++ b/solution.py
@@ -25,40 +25,26 @@
 OW = T // OUT_CHUNKS
 
 
-def peer(me, k):
-    step = k // 8
-    half = (step + 1) // 2
-    far = jnp.where(step % 2 == 1, half, Z - half)
-    dz = lax.rem(4 + far, Z)
-    dx = (k // 2 + 2) % X
-    dc = k % 2
+def others(me, fn):
     c = lax.rem(me, C)
     z = lax.rem(lax.div(me, C), Z)
     x = lax.div(me, C * Z)
-    return (lax.rem(x + dx, X) * Z + lax.rem(z + dz, Z)) * C + lax.rem(c + dc, C)
-
-
-def others(me, fn):
-    def one(k, carry):
-        d = peer(me, k)
-        fn(d)
-        return carry
-
-    own = SELF
-    lax.fori_loop(0, own, one, 0)
-    lax.fori_loop(own + 1, N, one, 0)
-
-
-def find_self():
-    for k in range(N):
-        step = k // 8
-        half = (step + 1) // 2
-        far = half if step % 2 == 1 else Z - half
-        if (4 + far) % Z == 0 and (k // 2 + 2) % X == 0 and k % 2 == 0:
-            return k
-
-
-SELF = find_self()
+    near = [
+        lax.rem(x + dx, X) * (Z * C) + lax.rem(c + dc, C)
+        for dx, dc in ((2, 0), (2, 1), (1, 0), (1, 1), (3, 0), (3, 1), (0, 1), (0, 0))
+    ]
+
+    def far(k, carry):
+        half = (k + 1) // 2
+        dz = jnp.where(k % 2 == 1, half, Z - half)
+        row = lax.rem(z + 4 + dz, Z) * C
+        for there in near:
+            fn(there + row)
+        return carry
+
+    lax.fori_loop(0, Z - 1, far, 0)
+    for there in near[:-1]:
+        fn(there + z * C)
 
 
 def exchange_kernel(

time: 82 us -> 79.8 us (0.973)
  Pallas kernels: 81.3 us -> 79 us
    pallas_call x1, Pallas kernels: 77.9 us -> 75.7 us  [body(): pl.pallas_call(exchange_kernel, out_shape=[pltpu.VMEM((Q, OUT_CHUNKS, BAN...]
where the time goes in v3:
time: 79.8 us; the launch traced here: 79.7 us
  Pallas kernels  79 us (99%)
    pallas_call x1, Pallas kernels, body(): pl.pallas_call(exchange_kernel, out_shape=[pltpu.VMEM((Q, OUT_CHUNKS, BAN...  75.7 us
    pallas_call x1, Pallas kernels, body(): pl.pallas_call(finish_kernel, out_shape=[jax.ShapeDtypeStruct((BANDS, R,...  3.35 us

profile of v3, /device:TPU:1, one launch (start us, length us, event | category | flops | bytes accessed | tf_op | source)
XLA Modules:
  0.0 79.7 jit_solution(12632769323884348645)
XLA Ops:
  0.6 75.7 %shard_map.102 = (bf16[4,4,16,8,512]{4,3,2,1,0:T(8,128)(2,1)S(1)}, bf16[16,8,2048]{2,1,0:T(8,128)(2,1)S(1)}, f32[2,512,512]{2,1,0:T(8,128)S(1)}, f32[2,512,512]{2,1,0:T(8,128)S(1)}) custom-call(s32[1,256]{1,0:T(1,128)} %bitcast.7, s32[1,256]{1,0:T(1,128)} %bitcast.8, s32[1,256]{1,0:T(1,128)} %bitcast.9, bf16[16,8,2048]{2,1,0:T(8,128)(2,1)} %g_hbm.1, ...), custom_call_target="tpu_custom_call" | custom-call | tf_op jit(solution)/shard_map/pallas_call | solution.py:307
  76.3 3.4 %shard_map.103 = (bf16[16,8,8192]{2,1,0:T(8,128)(2,1)}, bf16[16,8,2048]{2,1,0:T(8,128)(2,1)}, f32[1,1,2,512,512]{4,3,2,1,0:T(8,128)}, f32[1,1,2,512,512]{4,3,2,1,0:T(8,128)}) custom-call(bf16[4,4,16,8,512]{4,3,2,1,0:T(8,128)(2,1)S(1)} %get-tuple-element.8.y_all, bf16[16,8,2048]{2,1,0:T(8,128)(2,1)S(1)} %get-tuple-element.9.moment, ...), custom_call_target="tpu_custom_call" | custom-call | tf_op jit(solution)/shard_map/pallas_call | solution.py:351

commit v4 on v3

v4 whole, which is shorter than its diff:
```python
import functools

import jax
import jax.numpy as jnp
from jax import lax
from jax.experimental import pallas as pl
from jax.experimental.pallas import tpu as pltpu
from jax.sharding import PartitionSpec as P

MESH = pl.DeviceIdType.MESH
F32 = jnp.float32
BF16 = jnp.bfloat16

N = 64
X, Z, C = 4, 8, 2
Q = 4
T = 512
BANDS = 16
R = 8
W = 2048
NC = W // T
HW = T // 2
OUT_CHUNKS = 4
SINGLE = N - N // 4
STEP_BANDS = 2


def place(me):
    return lax.div(me, C * Z), lax.rem(lax.div(me, C), Z), lax.rem(me, C)


def near(me):
    x, _, c = place(me)
    return [
        lax.rem(x + dx, X) * (Z * C) + lax.rem(c + dc, C)
        for dx, dc in ((2, 0), (2, 1), (1, 0), (1, 1), (3, 0), (3, 1), (0, 1), (0, 0))
    ]


def others_far(me, fn, first, last):
    z = place(me)[1]
    same = near(me)

    def far(k, carry):
        half = (k + 1) // 2
        dz = jnp.where(k % 2 == 1, half, Z - half)
        row = lax.rem(z + 4 + dz, Z) * C
        for there in same:
            fn(there + row)
        return carry

    lax.fori_loop(first, last, far, 0)


def others_near(me, fn):
    z = place(me)[1]
    for there in near(me)[:-1]:
        fn(there + z * C)


def others(me, fn):
    others_far(me, fn, 0, Z - 1)
    others_near(me, fn)


def exchange_kernel(
    o_hbm, r0_hbm, c0_hbm, g_hbm, m_hbm, l_hbm, r_hbm, y_all, moment, left, right, table,
    where_v, idx_v, idx, gv, mv, lv, rv, pieces, apart, send_g, recv_g, grad, pre,
    send_u, ru0, ru1, ru2, ru3, sum_a, recv_a, sum_b, recv_b,
    load_sem, idx_sem, gs, gr, as_, ar, bs, br, us, ur, ys, yr,
):
    recv_u = (ru0, ru1, ru2, ru3)
    me = lax.axis_index("fsdp")
    mine = lax.axis_index("group")
    x, z, core = place(me)
    spot = x * C + core

    loads = [
        pltpu.make_async_copy(src, dst, load_sem.at[i])
        for i, (src, dst) in enumerate(
            [
                (g_hbm, gv), (m_hbm, mv), (l_hbm, lv), (r_hbm, rv),
                (o_hbm, where_v.at[0]), (r0_hbm, where_v.at[1]), (c0_hbm, where_v.at[2]),
            ]
        )
    ]
    for i in (4, 5, 6, 0, 1, 2, 3):
        loads[i].start()

    barrier = pltpu.get_barrier_semaphore()
    others(me, lambda d: pl.semaphore_signal(barrier, inc=1, device_id={"fsdp": d}, device_id_type=MESH))
    for k in range(1, Q):
        pl.semaphore_signal(
            barrier, inc=1, device_id={"group": lax.rem(mine + k, Q)}, device_id_type=MESH
        )

    for i in (4, 5, 6):
        loads[i].wait()
    row0, row1, owners, _ = positions(where_v, mine)
    idx_v[0:1] = row0
    idx_v[1:2] = row1
    idx_v[2:3] = owners
    to_smem = pltpu.make_async_copy(idx_v, idx, idx_sem)
    to_smem.start()

    loads[0].wait()

    def split(b, carry):
        rows = gv[b].astype(F32)
        for c in range(NC):
            for h in range(2):
                at = c * T + h * HW
                pieces[b * NC + c, h * R : (h + 1) * R] = rows[:, at : at + HW]
        return carry

    lax.fori_loop(0, BANDS, split, 0)
    pieces[N] = jnp.zeros((2 * R, HW), F32)
    to_smem.wait()

    def pack(o, carry):
        for s in range(2):
            send_g[s, o] = pieces[idx[s, o]].astype(BF16)
        return carry

    lax.fori_loop(0, N, pack, 0)

    pl.semaphore_wait(barrier, N - 1 + Q - 1)

    def send_slot(s):
        def send(d):
            pltpu.make_async_remote_copy(
                send_g.at[s, d], recv_g.at[s, me], gs.at[s], gr.at[s],
                device_id={"fsdp": d}, device_id_type=MESH,
            ).start()

        return send

    others(me, send_slot(0))

    loads[1].wait()

    def adam(b, carry):
        g = gv[b].astype(F32)
        m = mv[b].astype(F32)
        second = (0.95 * m + 0.05 * g * g).astype(BF16)
        moment[b] = second
        a = g / (jnp.sqrt(second.astype(F32)) + 1e-8)
        sq = a * a
        for c in range(NC):
            part = sq[:, c * T : c * T + 128]
            for i in range(1, T // 128):
                part = part + sq[:, c * T + i * 128 : c * T + (i + 1) * 128]
            apart[b * NC + c] = part
        return carry

    lax.fori_loop(0, BANDS, adam, 0)
    column = jnp.sum(jnp.sum(apart[...], axis=1), axis=1, keepdims=True)
    own_lane = lax.broadcasted_iota(jnp.int32, (N, 128), 0) == lax.broadcasted_iota(
        jnp.int32, (N, 128), 1
    )
    sum_a[...] = jnp.sum(jnp.where(own_lane, column, 0.0), axis=0, keepdims=True)
    recv_a[z] = sum_a[...]
    for dz in range(1, Z):
        pltpu.make_async_remote_copy(
            sum_a, recv_a.at[z], as_, ar,
            device_id={"fsdp": x * (Z * C) + lax.rem(z + dz, Z) * C + core}, device_id_type=MESH,
        ).start()
    others_far(me, send_slot(1), 0, 3)
    got = recv_a.at[pl.ds(0, Z - 1)]
    pltpu.make_async_copy(got, got, ar).wait()
    sum_b[...] = jnp.sum(recv_a[...], axis=0)
    recv_b[spot] = sum_b[...]

    def send_b(d):
        pltpu.make_async_remote_copy(
            sum_b, recv_b.at[spot], bs, br, device_id={"fsdp": d}, device_id_type=MESH
        ).start()

    others_near(me, send_b)
    others_far(me, send_slot(1), 3, Z - 1)
    others_near(me, send_slot(1))
    for s in range(2):
        recv_g[s, me] = send_g[s, me]

    loads[2].wait()
    loads[3].wait()

    group_rows = 8
    for s in range(2):
        got = recv_g.at[s, pl.ds(0, N - 1)]
        pltpu.make_async_copy(got, got, gr.at[s]).wait()

        def sort(t, carry, s=s):
            v = recv_g[s, pl.ds(t * group_rows, group_rows)].astype(F32)
            for h in range(2):
                rows = v[:, h * R : (h + 1) * R, :].reshape(group_rows * R, HW)
                grad[s, pl.ds(t * group_rows * R, group_rows * R), h * HW : (h + 1) * HW] = rows.astype(
                    BF16
                )
            return carry

        lax.fori_loop(0, N // group_rows, sort, 0)
        half = jnp.dot(lv[s], grad[s], preferred_element_type=F32).astype(BF16)
        pre[s] = jnp.dot(half, rv[s], preferred_element_type=F32)

        if s == 0:
            got = recv_b.at[pl.ds(0, X * C - 1)]
            pltpu.make_async_copy(got, got, br).wait()
            adam_sums = jnp.sum(recv_b[...], axis=0)
        lane = lax.broadcasted_iota(jnp.int32, (1, 128), 1)
        a_sum = jnp.sum(jnp.where(lane == idx[s, me], adam_sums, 0.0), axis=1, keepdims=True)
        sq = jnp.sum(pre[s] * pre[s], axis=0, keepdims=True)
        p_mean = jnp.sum(sq, axis=1, keepdims=True) / (T * T)
        scale = jnp.sqrt(a_sum / (T * T) / (p_mean + 1e-6))

        for h in range(2):
            j = s * 2 + h
            tiles = [
                (pre[s, :, pl.ds(h * HW + i * 128, 128)] * scale).reshape(N, R, 128) for i in range(2)
            ]
            send_u[j] = jnp.concatenate(tiles, axis=1).astype(BF16)

            def send(d, j=j):
                pltpu.make_async_remote_copy(
                    send_u.at[j, d], recv_u[j].at[me], us.at[j], ur.at[j],
                    device_id={"fsdp": d}, device_id_type=MESH,
                ).start()

            others(me, send)
            recv_u[j][me] = send_u[j, me]

    for s in range(2):
        g = grad[s]
        left[s] = (
            lax.dot_general(g, g, (((1,), (1,)), ((), ())), preferred_element_type=F32) / T
        )
        right[s] = (
            lax.dot_general(g, g, (((0,), (0,)), ((), ())), preferred_element_type=F32) / T
        )
    for q in range(Q):
        table[q : q + 1] = positions(where_v, q)[3]

    gathers = []
    for s, lo, hi in ((0, 0, SINGLE), (1, SINGLE, N)):
        for h in range(2):
            j = s * 2 + h
            got = recv_u[j].at[pl.ds(0, N - 1)]
            pltpu.make_async_copy(got, got, ur.at[j]).wait()

            def pick(k, carry, j=j, h=h, lo=lo):
                for e in range(4):
                    at = lo + k * 4 + e
                    t = recv_u[j][idx[2, at]].astype(F32)
                    y_all[mine, h, at] = jnp.concatenate([t[:R], t[R:]], axis=1).astype(BF16)
                return carry

            lax.fori_loop(0, (hi - lo) // 4, pick, 0)
            part = y_all.at[mine, h, pl.ds(lo, hi - lo)]
            for k in (2, 1, 3):
                copy = pltpu.make_async_remote_copy(
                    part, part, ys.at[j, k - 1], yr.at[j, k - 1],
                    device_id={"group": lax.rem(mine + k, Q)}, device_id_type=MESH,
                )
                copy.start()
                gathers.append(copy)

    for copy in gathers:
        copy.wait()
    for s in range(2):
        sent = send_g.at[s, pl.ds(0, N - 1)]
        pltpu.make_async_copy(sent, sent, gs.at[s]).wait()
    for j in range(OUT_CHUNKS):
        sent = send_u.at[j, pl.ds(0, N - 1)]
        pltpu.make_async_copy(sent, sent, us.at[j]).wait()
    sent = recv_a.at[pl.ds(0, Z - 1)]
    pltpu.make_async_copy(sent, sent, as_).wait()
    sent = recv_b.at[pl.ds(0, X * C - 1)]
    pltpu.make_async_copy(sent, sent, bs).wait()


def finish_kernel(
    y_all, moment, left, right, table, update_out, moment_out, left_out, right_out, rank, sem
):
    step = pl.program_id(0)
    copies = [
        pltpu.make_async_copy(left, left_out.at[0, 0], sem.at[0]),
        pltpu.make_async_copy(right, right_out.at[0, 0], sem.at[1]),
        pltpu.make_async_copy(moment, moment_out, sem.at[2]),
    ]

    @pl.when(step == 0)
    def _():
        ranks = pltpu.make_async_copy(table, rank, sem.at[3])
        ranks.start()
        for copy in copies:
            copy.start()
        ranks.wait()

    for b in range(STEP_BANDS):
        for q in range(Q):
            for c in range(NC):
                at = rank[q, (step * STEP_BANDS + b) * NC + c]
                for h in range(2):
                    col = q * W + c * T + h * HW
                    update_out[b, :, col : col + HW] = y_all[q, h, at]

    @pl.when(step == BANDS // STEP_BANDS - 1)
    def _():
        for copy in copies:
            copy.wait()


def positions(where_v, q):
    owner, row, col = where_v[0], where_v[1], where_v[2]
    blocks = owner.shape[1]
    col = col // T
    piece = (row // T) * NC + col % NC
    here = (col // NC) == q
    code = lax.broadcasted_iota(jnp.int32, (1, blocks), 1) * N + piece
    owner = jnp.where(here, owner, N)
    match = owner == lax.broadcasted_iota(jnp.int32, (N, blocks), 0)
    first = jnp.min(jnp.where(match, code, 1 << 20), axis=1, keepdims=True)
    last = jnp.max(jnp.where(match, code, -1), axis=1, keepdims=True)
    has0 = last >= 0
    has1 = last > first
    p0 = jnp.where(has0, first % N, N)
    p1 = jnp.where(has1, last % N, N)
    sub = lax.broadcasted_iota(jnp.int32, (N, 128), 0)
    lane = lax.broadcasted_iota(jnp.int32, (N, 128), 1)

    def total(v):
        return jnp.sum(v, axis=0, keepdims=True)

    row0 = total(jnp.where(sub == lane, p0, 0))
    row1 = total(jnp.where(sub == lane, p1, 0))

    def before(row):
        return jnp.sum(jnp.where((lane < sub) & (row < N), 1, 0), axis=1, keepdims=True)

    rank0 = jnp.where(has0, before(row0), -1)
    rank1 = jnp.where(has1, SINGLE + before(row1), -1)
    owners = total(jnp.where((rank0 == lane) | (rank1 == lane), sub, 0))
    ranks = total(jnp.where(p0 == lane, rank0, 0) + jnp.where(p1 == lane, rank1, 0))
    return row0, row1, owners, ranks


def body(gradient, second_moment, left_root, right_root, block_owner, row_offset, col_offset):
    hbm = pl.BlockSpec(memory_space=pltpu.HBM)
    vmem = pl.BlockSpec(memory_space=pltpu.VMEM)
    dma = pltpu.SemaphoreType.DMA
    blocks = block_owner.shape[0]
    places = [v.reshape(1, blocks) for v in (block_owner, row_offset, col_offset)]
    operands = [
        pltpu.with_memory_space_constraint(v, pltpu.HBM)
        for v in (*places, gradient, second_moment, left_root[0, 0], right_root[0, 0])
    ]
    kept = pl.pallas_call(
        exchange_kernel,
        out_shape=[
            pltpu.VMEM((Q, 2, N, R, HW), BF16),
            pltpu.VMEM((BANDS, R, W), BF16),
            pltpu.VMEM((2, T, T), F32),
            pltpu.VMEM((2, T, T), F32),
            pltpu.VMEM((8, 128), jnp.int32),
        ],
        in_specs=[hbm] * 7,
        out_specs=[vmem] * 5,
        scratch_shapes=[
            pltpu.VMEM((3, 1, blocks), jnp.int32),
            pltpu.VMEM((8, 128), jnp.int32),
            pltpu.SMEM((8, 128), jnp.int32),
            pltpu.VMEM((BANDS, R, W), BF16),
            pltpu.VMEM((BANDS, R, W), BF16),
            pltpu.VMEM((2, T, T), BF16),
            pltpu.VMEM((2, T, T), BF16),
            pltpu.VMEM((N + 1, 2 * R, HW), F32),
            pltpu.VMEM((N, R, 128), F32),
            pltpu.VMEM((2, N, 2 * R, HW), BF16),
            pltpu.VMEM((2, N, 2 * R, HW), BF16),
            pltpu.VMEM((2, T, T), BF16),
            pltpu.VMEM((2, T, T), F32),
            pltpu.VMEM((OUT_CHUNKS, N, 2 * R, 128), BF16),
            *[pltpu.VMEM((N, 2 * R, 128), BF16)] * OUT_CHUNKS,
            pltpu.VMEM((1, 128), F32),
            pltpu.VMEM((Z, 1, 128), F32),
            pltpu.VMEM((1, 128), F32),
            pltpu.VMEM((X * C, 1, 128), F32),
            dma((7,)),
            dma,
            dma((2,)),
            dma((2,)),
            dma,
            dma,
            dma,
            dma,
            dma((OUT_CHUNKS,)),
            dma((OUT_CHUNKS,)),
            dma((OUT_CHUNKS, Q - 1)),
            dma((OUT_CHUNKS, Q - 1)),
        ],
        compiler_params=pltpu.CompilerParams(
            collective_id=0, has_side_effects=True, vmem_limit_bytes=32 << 20
        ),
    )(*operands)

    return pl.pallas_call(
        finish_kernel,
        grid=(BANDS // STEP_BANDS,),
        out_shape=[
            jax.ShapeDtypeStruct((BANDS, R, Q * W), BF16),
            jax.ShapeDtypeStruct((BANDS, R, W), BF16),
            jax.ShapeDtypeStruct((1, 1, 2, T, T), F32),
            jax.ShapeDtypeStruct((1, 1, 2, T, T), F32),
        ],
        in_specs=[vmem] * 5,
        out_specs=[pl.BlockSpec((STEP_BANDS, R, Q * W), lambda t: (t, 0, 0)), hbm, hbm, hbm],
        scratch_shapes=[pltpu.SMEM((8, 128), jnp.int32), dma((4,))],
        compiler_params=pltpu.CompilerParams(vmem_limit_bytes=16 << 20),
    )(*kept)


def solution(mesh):
    placed = P(None, "fsdp", "group")
    slots = P("fsdp", "group", None, None, None)
    return jax.shard_map(
        body,
        mesh=mesh,
        in_specs=(placed, placed, slots, slots, P(), P(), P()),
        out_specs=(P(None, "fsdp", None), placed, slots, slots),
        check_vma=False,
    )
```

time: 79.8 us -> 74.2 us (0.930)
  Pallas kernels: 79 us -> 73.5 us
    pallas_call x2, Pallas kernels: 79 us -> 73.5 us  [the longest x1 68.9 us: body(): pl.pallas_call(exchange_kernel, out_shape=[pltpu.VMEM((Q, 2, N, R, HW), B...]
where the time goes in v4:
time: 74.2 us; the launch traced here: 74.1 us
  Pallas kernels  73.5 us (99%)
    pallas_call x1, Pallas kernels, body(): pl.pallas_call(exchange_kernel, out_shape=[pltpu.VMEM((Q, 2, N, R, HW), B...  68.9 us
    pallas_call x1, Pallas kernels, body(): pl.pallas_call(finish_kernel, grid=(BANDS // STEP_BANDS,), out_shape=[jax...  4.64 us

profile of v4, /device:TPU:1, one launch (start us, length us, event | category | flops | bytes accessed | tf_op | source)
XLA Modules:
  0.0 74.1 jit_solution(8005056141557544930)
XLA Ops:
  0.6 68.9 %shard_map.102 = (bf16[4,2,64,8,256]{4,3,2,1,0:T(8,128)(2,1)S(1)}, bf16[16,8,2048]{2,1,0:T(8,128)(2,1)S(1)}, f32[2,512,512]{2,1,0:T(8,128)S(1)}, f32[2,512,512]{2,1,0:T(8,128)S(1)}, s32[8,128]{1,0:T(8,128)S(1)}) custom-call(s32[1,256]{1,0:T(1,128)} %bitcast.7, s32[1,256]{1,0:T(1,128)} %bitcast.8, s32[1,256]{1,0:T(1,128)} %bitcast.9, ...), custom_call_target="tpu_custom_call" | custom-call | tf_op jit(solution)/shard_map/pallas_call | solution.py:357
  69.5 4.6 %shard_map.103 = (bf16[16,8,8192]{2,1,0:T(8,128)(2,1)}, bf16[16,8,2048]{2,1,0:T(8,128)(2,1)}, f32[1,1,2,512,512]{4,3,2,1,0:T(8,128)}, f32[1,1,2,512,512]{4,3,2,1,0:T(8,128)}) custom-call(bf16[4,2,64,8,256]{4,3,2,1,0:T(8,128)(2,1)S(1)} %get-tuple-element.9.y_all, bf16[16,8,2048]{2,1,0:T(8,128)(2,1)S(1)} %get-tuple-element.10.moment, ...), custom_call_target="tpu_custom_call" | custom-call | tf_op jit(solution)/shard_map/pallas_call | solution.py:406

commit v5 on v4

--- a/solution.py
+++ b/solution.py
@@ -22,7 +22,7 @@
 HW = T // 2
 OUT_CHUNKS = 4
 SINGLE = N - N // 4
-STEP_BANDS = 2
+STEP_BANDS = 4
 
 
 def place(me):
@@ -65,7 +65,7 @@
 
 def exchange_kernel(
     o_hbm, r0_hbm, c0_hbm, g_hbm, m_hbm, l_hbm, r_hbm, y_all, moment, left, right, table,
-    where_v, idx_v, idx, gv, mv, lv, rv, pieces, apart, send_g, recv_g, grad, pre,
+    where_v, idx_v, idx, table_v, gv, mv, lv, rv, pieces, apart, send_g, recv_g, grad, pre,
     send_u, ru0, ru1, ru2, ru3, sum_a, recv_a, sum_b, recv_b,
     load_sem, idx_sem, gs, gr, as_, ar, bs, br, us, ur, ys, yr,
 ):
@@ -88,7 +88,11 @@
         loads[i].start()
 
     barrier = pltpu.get_barrier_semaphore()
-    others(me, lambda d: pl.semaphore_signal(barrier, inc=1, device_id={"fsdp": d}, device_id_type=MESH))
+
+    def greet(d):
+        pl.semaphore_signal(barrier, inc=1, device_id={"fsdp": d}, device_id_type=MESH)
+
+    others_far(me, greet, 0, 4)
     for k in range(1, Q):
         pl.semaphore_signal(
             barrier, inc=1, device_id={"group": lax.rem(mine + k, Q)}, device_id_type=MESH
@@ -96,12 +100,13 @@
 
     for i in (4, 5, 6):
         loads[i].wait()
-    row0, row1, owners, _ = positions(where_v, mine)
+    row0, row1, _, _ = positions(where_v, mine)
     idx_v[0:1] = row0
     idx_v[1:2] = row1
-    idx_v[2:3] = owners
     to_smem = pltpu.make_async_copy(idx_v, idx, idx_sem)
     to_smem.start()
+    others_far(me, greet, 4, Z - 1)
+    others_near(me, greet)
 
     loads[0].wait()
 
@@ -117,12 +122,16 @@
     pieces[N] = jnp.zeros((2 * R, HW), F32)
     to_smem.wait()
 
-    def pack(o, carry):
-        for s in range(2):
-            send_g[s, o] = pieces[idx[s, o]].astype(BF16)
-        return carry
-
-    lax.fori_loop(0, N, pack, 0)
+    def pack(s):
+        def four(k, carry):
+            for e in range(4):
+                o = k * 4 + e
+                send_g[s, o] = pieces[idx[s, o]].astype(BF16)
+            return carry
+
+        lax.fori_loop(0, N // 4, four, 0)
+
+    pack(0)
 
     pl.semaphore_wait(barrier, N - 1 + Q - 1)
 
@@ -136,6 +145,7 @@
         return send
 
     others(me, send_slot(0))
+    pack(1)
 
     loads[1].wait()
 
@@ -238,9 +248,35 @@
             lax.dot_general(g, g, (((0,), (0,)), ((), ())), preferred_element_type=F32) / T
         )
     for q in range(Q):
-        table[q : q + 1] = positions(where_v, q)[3]
+        table_v[q : q + 1] = positions(where_v, q)[3]
+    table_v[Q : Q + 1] = positions(where_v, mine)[2]
+    to_table = pltpu.make_async_copy(table_v, table, idx_sem)
+    to_table.start()
+    to_table.wait()
 
     gathers = []
+    relays = []
+
+    def send_y(part, j, way, k):
+        copy = pltpu.make_async_remote_copy(
+            part, part, ys.at[j, way], yr.at[j, way],
+            device_id={"group": lax.rem(mine + k, Q)}, device_id_type=MESH,
+        )
+        copy.start()
+        return copy
+
+    def forward():
+        for j, h, right_copy, left_copy in relays:
+            right_copy.wait_recv()
+            gathers.append(send_y(y_all.at[lax.rem(mine + 3, Q), h, pl.ds(0, SINGLE // 2)], j, 2, 1))
+            left_copy.wait_recv()
+            gathers.append(
+                send_y(y_all.at[lax.rem(mine + 1, Q), h, pl.ds(SINGLE // 2, SINGLE // 2)], j, 3, 3)
+            )
+            right_copy.wait_send()
+            left_copy.wait_send()
+        relays.clear()
+
     for s, lo, hi in ((0, 0, SINGLE), (1, SINGLE, N)):
         for h in range(2):
             j = s * 2 + h
@@ -250,19 +286,19 @@
             def pick(k, carry, j=j, h=h, lo=lo):
                 for e in range(4):
                     at = lo + k * 4 + e
-                    t = recv_u[j][idx[2, at]].astype(F32)
+                    t = recv_u[j][table[Q, at]].astype(F32)
                     y_all[mine, h, at] = jnp.concatenate([t[:R], t[R:]], axis=1).astype(BF16)
                 return carry
 
             lax.fori_loop(0, (hi - lo) // 4, pick, 0)
             part = y_all.at[mine, h, pl.ds(lo, hi - lo)]
-            for k in (2, 1, 3):
-                copy = pltpu.make_async_remote_copy(
-                    part, part, ys.at[j, k - 1], yr.at[j, k - 1],
-                    device_id={"group": lax.rem(mine + k, Q)}, device_id_type=MESH,
-                )
-                copy.start()
-                gathers.append(copy)
+            if s == 0:
+                forward()
+                relays.append((j, h, send_y(part, j, 0, 1), send_y(part, j, 1, 3)))
+            else:
+                if h == 0:
+                    forward()
+                gathers.extend(send_y(part, j, way, k) for way, k in enumerate((2, 1, 3)))
 
     for copy in gathers:
         copy.wait()
@@ -279,7 +315,7 @@
 
 
 def finish_kernel(
-    y_all, moment, left, right, table, update_out, moment_out, left_out, right_out, rank, sem
+    y_all, moment, left, right, rank, update_out, moment_out, left_out, right_out, sem
 ):
     step = pl.program_id(0)
     copies = [
@@ -290,11 +326,8 @@
 
     @pl.when(step == 0)
     def _():
-        ranks = pltpu.make_async_copy(table, rank, sem.at[3])
-        ranks.start()
         for copy in copies:
             copy.start()
-        ranks.wait()
 
     for b in range(STEP_BANDS):
         for q in range(Q):
@@ -347,6 +380,7 @@
 def body(gradient, second_moment, left_root, right_root, block_owner, row_offset, col_offset):
     hbm = pl.BlockSpec(memory_space=pltpu.HBM)
     vmem = pl.BlockSpec(memory_space=pltpu.VMEM)
+    smem = pl.BlockSpec(memory_space=pltpu.SMEM)
     dma = pltpu.SemaphoreType.DMA
     blocks = block_owner.shape[0]
     places = [v.reshape(1, blocks) for v in (block_owner, row_offset, col_offset)]
@@ -361,14 +395,15 @@
             pltpu.VMEM((BANDS, R, W), BF16),
             pltpu.VMEM((2, T, T), F32),
             pltpu.VMEM((2, T, T), F32),
-            pltpu.VMEM((8, 128), jnp.int32),
+            pltpu.SMEM((8, 128), jnp.int32),
         ],
         in_specs=[hbm] * 7,
-        out_specs=[vmem] * 5,
+        out_specs=[vmem] * 4 + [smem],
         scratch_shapes=[
             pltpu.VMEM((3, 1, blocks), jnp.int32),
             pltpu.VMEM((8, 128), jnp.int32),
             pltpu.SMEM((8, 128), jnp.int32),
+            pltpu.VMEM((8, 128), jnp.int32),
             pltpu.VMEM((BANDS, R, W), BF16),
             pltpu.VMEM((BANDS, R, W), BF16),
             pltpu.VMEM((2, T, T), BF16),
@@ -395,8 +430,8 @@
             dma,
             dma((OUT_CHUNKS,)),
             dma((OUT_CHUNKS,)),
-            dma((OUT_CHUNKS, Q - 1)),
-            dma((OUT_CHUNKS, Q - 1)),
+            dma((OUT_CHUNKS, Q)),
+            dma((OUT_CHUNKS, Q)),
         ],
         compiler_params=pltpu.CompilerParams(
             collective_id=0, has_side_effects=True, vmem_limit_bytes=32 << 20
@@ -412,9 +447,9 @@
             jax.ShapeDtypeStruct((1, 1, 2, T, T), F32),
             jax.ShapeDtypeStruct((1, 1, 2, T, T), F32),
         ],
-        in_specs=[vmem] * 5,
+        in_specs=[vmem] * 4 + [smem],
         out_specs=[pl.BlockSpec((STEP_BANDS, R, Q * W), lambda t: (t, 0, 0)), hbm, hbm, hbm],
-        scratch_shapes=[pltpu.SMEM((8, 128), jnp.int32), dma((4,))],
+        scratch_shapes=[dma((3,))],
         compiler_params=pltpu.CompilerParams(vmem_limit_bytes=16 << 20),
     )(*kept)
 

time: 74.2 us -> 70.5 us (0.950)
  Pallas kernels: 73.5 us -> 69.6 us
    pallas_call x1, Pallas kernels: 68.9 us -> 66.2 us  [body(): pl.pallas_call(exchange_kernel, out_shape=[pltpu.VMEM((Q, 2, N, R, HW), B...]
    pallas_call x1, Pallas kernels: 4.64 us -> 3.44 us  [body(): pl.pallas_call(finish_kernel, grid=(BANDS // STEP_BANDS,), out_shape=[jax...]
where the time goes in v5:
time: 70.5 us; the launch traced here: 70.3 us
  Pallas kernels  69.6 us (99%)
    pallas_call x1, Pallas kernels, body(): pl.pallas_call(exchange_kernel, out_shape=[pltpu.VMEM((Q, 2, N, R, HW), B...  66.2 us
    pallas_call x1, Pallas kernels, body(): pl.pallas_call(finish_kernel, grid=(BANDS // STEP_BANDS,), out_shape=[jax...  3.44 us

profile of v5, /device:TPU:1, one launch (start us, length us, event | category | flops | bytes accessed | tf_op | source)
XLA Modules:
  0.0 70.3 jit_solution(13598627992449485812)
XLA Ops:
  0.6 66.2 %shard_map.102 = (bf16[4,2,64,8,256]{4,3,2,1,0:T(8,128)(2,1)S(1)}, bf16[16,8,2048]{2,1,0:T(8,128)(2,1)S(1)}, f32[2,512,512]{2,1,0:T(8,128)S(1)}, f32[2,512,512]{2,1,0:T(8,128)S(1)}, s32[8,128]{1,0:T(8,128)S(4)}) custom-call(s32[1,256]{1,0:T(1,128)} %bitcast.7, s32[1,256]{1,0:T(1,128)} %bitcast.8, s32[1,256]{1,0:T(1,128)} %bitcast.9, ...), custom_call_target="tpu_custom_call" | custom-call | tf_op jit(solution)/shard_map/pallas_call | solution.py:391
  66.8 3.4 %shard_map.103 = (bf16[16,8,8192]{2,1,0:T(8,128)(2,1)}, bf16[16,8,2048]{2,1,0:T(8,128)(2,1)}, f32[1,1,2,512,512]{4,3,2,1,0:T(8,128)}, f32[1,1,2,512,512]{4,3,2,1,0:T(8,128)}) custom-call(bf16[4,2,64,8,256]{4,3,2,1,0:T(8,128)(2,1)S(1)} %get-tuple-element.9.y_all, bf16[16,8,2048]{2,1,0:T(8,128)(2,1)S(1)} %get-tuple-element.10.moment, ...), custom_call_target="tpu_custom_call" | custom-call | tf_op jit(solution)/shard_map/pallas_call | solution.py:441

commit v6 on v5

--- a/solution.py
+++ b/solution.py
@@ -22,7 +22,8 @@
 HW = T // 2
 OUT_CHUNKS = 4
 SINGLE = N - N // 4
-STEP_BANDS = 4
+STEP_BANDS = 8
+EARLY = 7
 
 
 def place(me):
@@ -175,7 +176,7 @@
             sum_a, recv_a.at[z], as_, ar,
             device_id={"fsdp": x * (Z * C) + lax.rem(z + dz, Z) * C + core}, device_id_type=MESH,
         ).start()
-    others_far(me, send_slot(1), 0, 3)
+    others_far(me, send_slot(1), 0, 4)
     got = recv_a.at[pl.ds(0, Z - 1)]
     pltpu.make_async_copy(got, got, ar).wait()
     sum_b[...] = jnp.sum(recv_a[...], axis=0)
@@ -187,8 +188,15 @@
         ).start()
 
     others_near(me, send_b)
-    others_far(me, send_slot(1), 3, Z - 1)
+    others_far(me, send_slot(1), 4, Z - 1)
     others_near(me, send_slot(1))
+    for q in range(Q):
+        table_v[q : q + 1] = positions(where_v, q)[3]
+    table_v[Q : Q + 1] = positions(where_v, mine)[2]
+    to_table = pltpu.make_async_copy(table_v, table, idx_sem)
+    to_table.start()
+    to_table.wait()
+
     for s in range(2):
         recv_g[s, me] = send_g[s, me]
 
@@ -196,11 +204,12 @@
     loads[3].wait()
 
     group_rows = 8
-    for s in range(2):
+
+    def take(s):
         got = recv_g.at[s, pl.ds(0, N - 1)]
         pltpu.make_async_copy(got, got, gr.at[s]).wait()
 
-        def sort(t, carry, s=s):
+        def sort(t, carry):
             v = recv_g[s, pl.ds(t * group_rows, group_rows)].astype(F32)
             for h in range(2):
                 rows = v[:, h * R : (h + 1) * R, :].reshape(group_rows * R, HW)
@@ -213,46 +222,28 @@
         half = jnp.dot(lv[s], grad[s], preferred_element_type=F32).astype(BF16)
         pre[s] = jnp.dot(half, rv[s], preferred_element_type=F32)
 
-        if s == 0:
-            got = recv_b.at[pl.ds(0, X * C - 1)]
-            pltpu.make_async_copy(got, got, br).wait()
-            adam_sums = jnp.sum(recv_b[...], axis=0)
+    def graft(s, adam_sums):
         lane = lax.broadcasted_iota(jnp.int32, (1, 128), 1)
         a_sum = jnp.sum(jnp.where(lane == idx[s, me], adam_sums, 0.0), axis=1, keepdims=True)
         sq = jnp.sum(pre[s] * pre[s], axis=0, keepdims=True)
         p_mean = jnp.sum(sq, axis=1, keepdims=True) / (T * T)
-        scale = jnp.sqrt(a_sum / (T * T) / (p_mean + 1e-6))
-
-        for h in range(2):
-            j = s * 2 + h
-            tiles = [
-                (pre[s, :, pl.ds(h * HW + i * 128, 128)] * scale).reshape(N, R, 128) for i in range(2)
-            ]
-            send_u[j] = jnp.concatenate(tiles, axis=1).astype(BF16)
-
-            def send(d, j=j):
-                pltpu.make_async_remote_copy(
-                    send_u.at[j, d], recv_u[j].at[me], us.at[j], ur.at[j],
-                    device_id={"fsdp": d}, device_id_type=MESH,
-                ).start()
-
-            others(me, send)
-            recv_u[j][me] = send_u[j, me]
-
-    for s in range(2):
-        g = grad[s]
-        left[s] = (
-            lax.dot_general(g, g, (((1,), (1,)), ((), ())), preferred_element_type=F32) / T
-        )
-        right[s] = (
-            lax.dot_general(g, g, (((0,), (0,)), ((), ())), preferred_element_type=F32) / T
-        )
-    for q in range(Q):
-        table_v[q : q + 1] = positions(where_v, q)[3]
-    table_v[Q : Q + 1] = positions(where_v, mine)[2]
-    to_table = pltpu.make_async_copy(table_v, table, idx_sem)
-    to_table.start()
-    to_table.wait()
+        return jnp.sqrt(a_sum / (T * T) / (p_mean + 1e-6))
+
+    def send_back(s, h, scale):
+        j = s * 2 + h
+        tiles = [
+            (pre[s, :, pl.ds(h * HW + i * 128, 128)] * scale).reshape(N, R, 128) for i in range(2)
+        ]
+        send_u[j] = jnp.concatenate(tiles, axis=1).astype(BF16)
+
+        def send(d):
+            pltpu.make_async_remote_copy(
+                send_u.at[j, d], recv_u[j].at[me], us.at[j], ur.at[j],
+                device_id={"fsdp": d}, device_id_type=MESH,
+            ).start()
+
+        others(me, send)
+        recv_u[j][me] = send_u[j, me]
 
     gathers = []
     relays = []
@@ -277,28 +268,51 @@
             left_copy.wait_send()
         relays.clear()
 
-    for s, lo, hi in ((0, 0, SINGLE), (1, SINGLE, N)):
-        for h in range(2):
-            j = s * 2 + h
-            got = recv_u[j].at[pl.ds(0, N - 1)]
-            pltpu.make_async_copy(got, got, ur.at[j]).wait()
-
-            def pick(k, carry, j=j, h=h, lo=lo):
-                for e in range(4):
-                    at = lo + k * 4 + e
-                    t = recv_u[j][table[Q, at]].astype(F32)
-                    y_all[mine, h, at] = jnp.concatenate([t[:R], t[R:]], axis=1).astype(BF16)
-                return carry
-
-            lax.fori_loop(0, (hi - lo) // 4, pick, 0)
-            part = y_all.at[mine, h, pl.ds(lo, hi - lo)]
-            if s == 0:
-                forward()
-                relays.append((j, h, send_y(part, j, 0, 1), send_y(part, j, 1, 3)))
-            else:
-                if h == 0:
-                    forward()
-                gathers.extend(send_y(part, j, way, k) for way, k in enumerate((2, 1, 3)))
+    def gather(s, h):
+        j = s * 2 + h
+        lo, hi = (0, SINGLE) if s == 0 else (SINGLE, N)
+        got = recv_u[j].at[pl.ds(0, N - 1)]
+        pltpu.make_async_copy(got, got, ur.at[j]).wait()
+
+        def pick(k, carry):
+            for e in range(4):
+                at = lo + k * 4 + e
+                t = recv_u[j][table[Q, at]].astype(F32)
+                y_all[mine, h, at] = jnp.concatenate([t[:R], t[R:]], axis=1).astype(BF16)
+            return carry
+
+        lax.fori_loop(0, (hi - lo) // 4, pick, 0)
+        part = y_all.at[mine, h, pl.ds(lo, hi - lo)]
+        if s == 0:
+            relays.append((j, h, send_y(part, j, 0, 1), send_y(part, j, 1, 3)))
+        else:
+            gathers.extend(send_y(part, j, way, k) for way, k in enumerate((2, 1, 3)))
+
+    take(0)
+    got = recv_b.at[pl.ds(0, X * C - 1)]
+    pltpu.make_async_copy(got, got, br).wait()
+    adam_sums = jnp.sum(recv_b[...], axis=0)
+    scale = graft(0, adam_sums)
+    send_back(0, 0, scale)
+    send_back(0, 1, scale)
+    take(1)
+    scale = graft(1, adam_sums)
+    send_back(1, 0, scale)
+    send_back(1, 1, scale)
+    for s in range(2):
+        g = grad[s]
+        left[s] = (
+            lax.dot_general(g, g, (((1,), (1,)), ((), ())), preferred_element_type=F32) / T
+        )
+        right[s] = (
+            lax.dot_general(g, g, (((0,), (0,)), ((), ())), preferred_element_type=F32) / T
+        )
+    gather(0, 0)
+    forward()
+    gather(0, 1)
+    gather(1, 0)
+    forward()
+    gather(1, 1)
 
     for copy in gathers:
         copy.wait()

time: 70.5 us -> 69 us (0.979)
  Pallas kernels: 69.6 us -> 68 us
    pallas_call x1, Pallas kernels: 66.2 us -> 64.7 us  [body(): pl.pallas_call(exchange_kernel, out_shape=[pltpu.VMEM((Q, 2, N, R, HW), B...]
where the time goes in v6:
time: 69 us; the launch traced here: 68.6 us
  Pallas kernels  68 us (99%)
    pallas_call x1, Pallas kernels, body(): pl.pallas_call(exchange_kernel, out_shape=[pltpu.VMEM((Q, 2, N, R, HW), B...  64.7 us
    pallas_call x1, Pallas kernels, body(): pl.pallas_call(finish_kernel, grid=(BANDS // STEP_BANDS,), out_shape=[jax...  3.21 us

profile of v6, /device:TPU:1, one launch (start us, length us, event | category | flops | bytes accessed | tf_op | source)
XLA Modules:
  0.0 68.6 jit_solution(13227497900720124519)
XLA Ops:
  0.6 64.7 %shard_map.102 = (bf16[4,2,64,8,256]{4,3,2,1,0:T(8,128)(2,1)S(1)}, bf16[16,8,2048]{2,1,0:T(8,128)(2,1)S(1)}, f32[2,512,512]{2,1,0:T(8,128)S(1)}, f32[2,512,512]{2,1,0:T(8,128)S(1)}, s32[8,128]{1,0:T(8,128)S(4)}) custom-call(s32[1,256]{1,0:T(1,128)} %bitcast.7, s32[1,256]{1,0:T(1,128)} %bitcast.8, s32[1,256]{1,0:T(1,128)} %bitcast.9, ...), custom_call_target="tpu_custom_call" | custom-call | tf_op jit(solution)/shard_map/pallas_call | solution.py:405
  65.4 3.2 %shard_map.103 = (bf16[16,8,8192]{2,1,0:T(8,128)(2,1)}, bf16[16,8,2048]{2,1,0:T(8,128)(2,1)}, f32[1,1,2,512,512]{4,3,2,1,0:T(8,128)}, f32[1,1,2,512,512]{4,3,2,1,0:T(8,128)}) custom-call(bf16[4,2,64,8,256]{4,3,2,1,0:T(8,128)(2,1)S(1)} %get-tuple-element.9.y_all, bf16[16,8,2048]{2,1,0:T(8,128)(2,1)S(1)} %get-tuple-element.10.moment, ...), custom_call_target="tpu_custom_call" | custom-call | tf_op jit(solution)/shard_map/pallas_call | solution.py:455

commit v7 on v6

--- a/solution.py
+++ b/solution.py
@@ -298,6 +298,7 @@
     take(1)
     scale = graft(1, adam_sums)
     send_back(1, 0, scale)
+    gather(0, 0)
     send_back(1, 1, scale)
     for s in range(2):
         g = grad[s]
@@ -307,7 +308,6 @@
         right[s] = (
             lax.dot_general(g, g, (((0,), (0,)), ((), ())), preferred_element_type=F32) / T
         )
-    gather(0, 0)
     forward()
     gather(0, 1)
     gather(1, 0)

time: 69 us -> 69 us (level)
  no operation moved by 1% of the time
where the time goes in v7:
time: 69 us; the launch traced here: 68.7 us
  Pallas kernels  68.1 us (99%)
    pallas_call x1, Pallas kernels, body(): pl.pallas_call(exchange_kernel, out_shape=[pltpu.VMEM((Q, 2, N, R, HW), B...  64.9 us
    pallas_call x1, Pallas kernels, body(): pl.pallas_call(finish_kernel, grid=(BANDS // STEP_BANDS,), out_shape=[jax...  3.21 us

profile of v7, /device:TPU:1, one launch (start us, length us, event | category | flops | bytes accessed | tf_op | source)
XLA Modules:
  0.0 68.7 jit_solution(13505724859467156607)
XLA Ops:
  0.6 64.9 %shard_map.102 = (bf16[4,2,64,8,256]{4,3,2,1,0:T(8,128)(2,1)S(1)}, bf16[16,8,2048]{2,1,0:T(8,128)(2,1)S(1)}, f32[2,512,512]{2,1,0:T(8,128)S(1)}, f32[2,512,512]{2,1,0:T(8,128)S(1)}, s32[8,128]{1,0:T(8,128)S(4)}) custom-call(s32[1,256]{1,0:T(1,128)} %bitcast.7, s32[1,256]{1,0:T(1,128)} %bitcast.8, s32[1,256]{1,0:T(1,128)} %bitcast.9, ...), custom_call_target="tpu_custom_call" | custom-call | tf_op jit(solution)/shard_map/pallas_call | solution.py:405
  65.5 3.2 %shard_map.103 = (bf16[16,8,8192]{2,1,0:T(8,128)(2,1)}, bf16[16,8,2048]{2,1,0:T(8,128)(2,1)}, f32[1,1,2,512,512]{4,3,2,1,0:T(8,128)}, f32[1,1,2,512,512]{4,3,2,1,0:T(8,128)}) custom-call(bf16[4,2,64,8,256]{4,3,2,1,0:T(8,128)(2,1)S(1)} %get-tuple-element.9.y_all, bf16[16,8,2048]{2,1,0:T(8,128)(2,1)S(1)} %get-tuple-element.10.moment, ...), custom_call_target="tpu_custom_call" | custom-call | tf_op jit(solution)/shard_map/pallas_call | solution.py:455
